TPU v7x, 512 devices: a whole 4x4x16 slice. The times are simulated.
512 devices in a mesh: row: 8 (over x, core), col: 64 (over y, z).
Axes of the slice: x: 4, y: 4, z: 16, core: 2. Of those that a mesh axis runs over, the one named last changes fastest.
Arguments:
- diag_factors: bfloat16 [3, 512, 512], replicated, as said below
- panel_v: bfloat16 [64, 2, 512, 128], P('row', None, 'col'), may hold values from -2.515625 to 2.515625
- ranks: int32 [64, 2], P('row'), may hold values from 32 to 128, as said below
Outputs:
- panel_factors: bfloat16 [64, 1024, 256], P('row', 'col')
- update_cores: float32 [64, 64, 256, 256], P('row', 'col')
Inputs may be any that keep to these rules, and one draw needn't show every extreme that they name: `ranks`: every panel tile has rank at least 32; the tiles of array row 0 have rank 128. `diag_factors`: inverse0 and inverse1 are lower triangular with positive diagonals.
All inputs are finite; a program needn't handle non-finite values.
Results may differ from a plain program's by a relative error of at most 0.0046.
Values may be sent and summed in bfloat16 or wider, within the bound.
No kernel may reach another device: no remote copies, remote signals or barrier semaphores. Data moves between devices by JAX's collectives and lax.ppermute only.
A program may use at most 64 MiB of HBM per device.

v0:
```python
import jax
import jax.numpy as jnp
from jax import lax
from jax.sharding import PartitionSpec as P


def from_root(block, axis, source):
    block = jnp.where(lax.axis_index(axis) == source, block, jnp.zeros_like(block))
    return lax.psum(block, axis)


def assemble(w_block, lower, right):
    top = jnp.concatenate([w_block, jnp.zeros_like(w_block)], axis=-1)
    bottom = jnp.concatenate([lower, right], axis=-1)
    return jnp.concatenate([top, bottom], axis=-2)


def shards(diag_factors, panel_v, ranks):
    rows_dev = panel_v.shape[0]
    rank_max = panel_v.shape[3]
    nrow = lax.axis_size("row")
    ncol = lax.axis_size("col")
    prow = lax.axis_index("row")
    qcol = lax.axis_index("col")
    inverse0 = diag_factors[0]
    couple = diag_factors[1]
    inverse1 = diag_factors[2]
    columns = jnp.arange(rank_max, dtype=jnp.int32)
    keep = columns[None, None, :] < ranks[:, :, None]
    masked = jnp.where(keep[:, :, None, :], panel_v, jnp.zeros_like(panel_v))
    whole = lax.all_gather(masked, "col", axis=2, tiled=True)
    w_block = jnp.einsum(
        "nm,tmr->tnr", inverse0, whole[:, 0], preferred_element_type=jnp.float32
    ).astype(jnp.bfloat16)
    right = jnp.einsum(
        "nm,tmr->tnr", inverse1, whole[:, 1], preferred_element_type=jnp.float32
    ).astype(jnp.bfloat16)
    lower = jnp.einsum("nm,tmr->tnr", couple, w_block, preferred_element_type=jnp.float32).astype(
        jnp.bfloat16
    )
    factors = assemble(w_block, lower, right)
    piece = factors.shape[1] // ncol
    factor_share = lax.dynamic_slice_in_dim(factors, qcol * piece, piece, 1)
    owner = qcol % nrow
    local_row = qcol // nrow
    picked = lax.dynamic_index_in_dim(factors, local_row, 0, keepdims=False)
    column_factor = from_root(picked, "row", owner)
    cores = jnp.einsum("tkr,ks->trs", factors, column_factor, preferred_element_type=jnp.float32)
    codes = jnp.arange(rows_dev, dtype=jnp.int32) * nrow + prow
    active = codes > qcol
    cores = jnp.where(active[:, None, None], cores, jnp.zeros_like(cores))
    return (factor_share, cores[:, None])


def solution(mesh):
    placed = (P(), P("row", None, "col", None), P("row", None))
    return jax.shard_map(
        shards,
        mesh=mesh,
        in_specs=placed,
        out_specs=(P("row", "col", None), P("row", "col", None, None)),
        check_vma=False,
    )
```

profile of v0, /device:TPU:1, one launch (start us, length us, event | category | flops | bytes accessed | tf_op | source)
XLA Modules:
  0.0 252.0 jit_solution(16143106622238425557)
XLA Ops:
  7.2 0.0 all-gather.2.cloned.1.call-start
  7.2 0.8 iota_compare_fusion.1
  8.0 1.4 copy_select_fusion
  9.3 0.0 all-gather.2.cloned.1.call-update
  9.4 0.0 all-reduce.3.cloned.1.call-start
  9.4 139.5 %all-gather.2.cloned.1.call-done = bf16[8,2,512,128]{3,0,1,2:T(8,128)(2,1)} async-done(((bf16[8,2,8,128]{3,0,1,2:T(8,128)(2,1)}), bf16[8,2,512,128]{3,0,1,2:T(8,128)(2,1)}) %all-gather.2.cloned.1.call-update) | async-done | bytes 2097168 | tf_op jit(solution)/shard_map/all_gather | solution.py:31
  149.0 1.7 fusion.15
  150.7 0.7 copy.17
  151.4 0.7 copy.18
  152.0 1.8 fusion.2
  153.8 1.8 fusion.4
  155.6 1.8 fusion.3
  157.4 0.0 copy-start.1
  157.4 1.0 copy-done.1
  158.4 0.5 fusion.1
  158.9 0.0 copy-start
  158.9 1.9 copy-done
  160.9 0.8 select_bitcast_fusion.1
  161.7 0.0 all-reduce.3.cloned.1.call-update
  161.7 1.3 constant_dynamic-slice_fusion
  163.0 0.8 copy.13
  163.8 77.4 %all-reduce.3.cloned.1.call-done = bf16[1024,256]{0,1:T(8,128)(2,1)} async-done(((bf16[1024,256]{0,1:T(8,128)(2,1)}), bf16[1024,256]{0,1:T(8,128)(2,1)}) %all-reduce.3.cloned.1.call-update) | async-done | bytes 524304 | tf_op jit(solution)/shard_map/psum | solution.py:9
  241.2 4.0 %select_bitcast_fusion = f32[8,1,256,256]{3,2,1,0:T(8,128)} fusion(pred[8]{0:T(512)(128)(4,1)S(1)} %add_compare_fusion, bf16[1024,256]{0,1:T(8,128)(2,1)} %all-reduce.3.cloned.1.call-done, bf16[8,512,128]{1,2,0:T(8,128)(2,1)S(1)} %fusion.2, bf16[8,512,128]{1,2,0:T(8,128)(2,1)S(1)} %fusion.4, bf16[8,512,128]{1,2,0:T(8,128)(2,1)} %copy-done.1), kind=kOutput, calls=%fused_computation.3 | convolution fusion | flops 1091043328 | bytes 5767176 | tf_op jit(solution)/shard_map/tkr,ks->trs/dot_general | solution.py:48
  (1 shorter events, 0.0 us)
Async XLA Ops:
  7.2 141.8 %all-gather.2.cloned.1.call-start = ((), (), s32[]{:S(2)}) async-start(), calls=%async_computation | async-start | bytes 2129920 | tf_op jit(solution)/shard_map/all_gather | solution.py:31
  9.4 231.9 %all-reduce.3.cloned.1.call-start = ((), (), s32[]{:S(2)}) async-start(), calls=%async_computation.1 | async-start | bytes 1048576 | tf_op jit(solution)/shard_map/psum | solution.py:9
  157.4 1.0 copy-start.1
  158.9 1.9 copy-start
Sparse Core Ops, SparseCore 0:
  11.5 137.4 all-gather.1
  161.8 79.3 all-reduce.2
where the time goes:
time: 253 us; the launch traced here: 252 us
  waiting for transfers between devices  217 us (86%)
  between operations  14.1 us (6%)
  matrix products  9.31 us (4%)
  local copies, waits for them, and re-layouts  8.01 us (3%)
  other arithmetic  3.49 us (1%)
    all_gather x1, waiting for transfers between devices, shards(): whole = lax.all_gather(masked, 'col', axis=2, tiled=True)  140 us
    psum x1, waiting for transfers between devices, from_root(): return lax.psum(block, axis)  77.4 us
    unnamed x7, local copies, waits for them, and re-layouts  5.07 us
  transfers between devices with their start and end apart: 2, of which 2 were waited for; matrix products, arithmetic and copies ran while one was open for 1% of the time, Pallas kernels for 0%

commit v1 on v0

v1 whole, which is shorter than its diff:
```python
import jax
import jax.numpy as jnp
from jax import lax
from jax.sharding import PartitionSpec as P

Y = 4
Z = 16


def dot(a, b, dims):
    return lax.dot_general(a, b, (dims, ((), ())), preferred_element_type=jnp.float32)


def shards(diag_factors, panel_v, ranks):
    tiles, pair, mine, rank = panel_v.shape
    nrow = lax.axis_size("row")
    prow = lax.axis_index("row")
    qcol = lax.axis_index("col")
    bf16 = jnp.bfloat16
    along_z = [[y * Z + z for z in range(Z)] for y in range(Y)]
    along_y = [[y * Z + z for y in range(Y)] for z in range(Z)]
    flat = panel_v.transpose(2, 0, 1, 3).reshape(mine, tiles * pair * rank)
    keep = jnp.arange(rank, dtype=jnp.int32)[None, None, :] < ranks[:, :, None]
    flat = jnp.where(keep.reshape(1, -1), flat, jnp.zeros_like(flat))
    slab = lax.all_gather(flat, "col", axis=0, tiled=True, axis_index_groups=along_z)
    sent = jnp.broadcast_to(slab[None], (Y,) + slab.shape)
    whole = lax.all_to_all(sent, "col", 0, 0, axis_index_groups=along_y)
    whole = whole.reshape(-1, flat.shape[1])
    nloc = whole.shape[0]
    wide = pair * rank
    picked = lax.dynamic_slice_in_dim(whole, (qcol // nrow) * wide, wide, 1)
    cut = lax.all_to_all(picked.reshape(nrow, nloc // nrow, wide), "row", 0, 0)
    cut = lax.dynamic_index_in_dim(cut, qcol % nrow, 0, keepdims=True)
    column = lax.all_to_all(jnp.broadcast_to(cut, (nrow,) + cut.shape[1:]), "row", 0, 0)
    column = column.reshape(nloc, wide)

    def factor(v):
        v = v.reshape(nloc, -1, pair, rank)
        w = dot(diag_factors[0], v[:, :, 0].reshape(nloc, -1), ((1,), (0,))).astype(bf16)
        right = dot(diag_factors[2], v[:, :, 1].reshape(nloc, -1), ((1,), (0,))).astype(bf16)
        lower = dot(diag_factors[1], w, ((1,), (0,))).astype(bf16)
        w, lower, right = (a.reshape(nloc, -1, 1, rank) for a in (w, lower, right))
        top = jnp.concatenate([w, jnp.zeros_like(w)], 2)
        bottom = jnp.concatenate([lower, right], 2)
        return jnp.concatenate([top, bottom], 0).reshape(2 * nloc, -1, wide)

    factors = factor(whole)
    mate = factor(column)[:, 0]
    piece = 2 * nloc // lax.axis_size("col")
    share = lax.dynamic_slice_in_dim(factors, qcol * piece, piece, 0).transpose(1, 0, 2)
    cores = jnp.einsum("ktr,ks->trs", factors, mate, preferred_element_type=jnp.float32)
    codes = jnp.arange(tiles, dtype=jnp.int32) * nrow + prow
    cores = jnp.where((codes > qcol)[:, None, None], cores, jnp.zeros_like(cores))
    return share, cores[:, None]


def solution(mesh):
    placed = (P(), P("row", None, "col", None), P("row", None))
    return jax.shard_map(
        shards,
        mesh=mesh,
        in_specs=placed,
        out_specs=(P("row", "col", None), P("row", "col", None, None)),
        check_vma=False,
    )
```

time: 253 us -> 110 us (0.43)
  waiting for transfers between devices: 217 us -> 19.9 us
  blocking collectives: 0 us -> 31.8 us
  starting transfers between devices: 0.08 us -> 23 us
  local copies, waits for them, and re-layouts: 8.01 us -> 25.6 us
  between operations: 14.1 us -> 0.82 us
    all_gather x1 -> x0, waiting for transfers between devices: 140 us -> none  [shards(): whole = lax.all_gather(masked, 'col', axis=2, tiled=True)]
    psum x1 -> x0, waiting for transfers between devices: 77.4 us -> none  [from_root(): return lax.psum(block, axis)]
    all_gather x0 -> x1, blocking collectives: none -> 31.8 us  [shards(): lax.all_gather(flat, 'col', axis=0, tiled=True, axis_index_groups=along_z)]
    all_to_all x0 -> x3, starting transfers between devices: none -> 23 us  [the longest x1 14 us: shards(): cut = lax.all_to_all(picked.reshape(nrow, nloc // nrow, wide), 'row', 0, 0)]
    all_to_all x0 -> x3, waiting for transfers between devices: none -> 19.9 us  [the longest x1 17.5 us: shards(): whole = lax.all_to_all(sent, 'col', 0, 0, axis_index_groups=along_y)]
    slice x1 -> x4, local copies, waits for them, and re-layouts: 1.68 us -> 13.4 us  [the longest x3 9.22 us: factor(): v[:, :, 1].reshape(nloc, -1)]
    another operation x0 -> x2, local copies, waits for them, and re-layouts: none -> 3.29 us  [factor(): v = v.reshape(nloc, -1, pair, rank)]
    dot_general x4 -> x7, matrix products: 9.31 us -> 6.99 us  [the longest x6 4.33 us: dot(): lax.dot_general(a, b, (dims, ((), ())), preferred_element_type=jnp.float32)]
  transfers between devices with their start and end apart: 2 -> 3, of which waited for: 2 -> 2; matrix products, arithmetic and copies ran while one was open for 1% -> 20% of each run, Pallas kernels for 0% -> 0%
where the time goes in v1:
time: 110 us
  blocking collectives  31.8 us (29%)
  local copies, waits for them, and re-layouts  25.6 us (23%)
  starting transfers between devices  23 us (21%)
  waiting for transfers between devices  19.9 us (18%)
  matrix products  6.99 us (6%)
  other arithmetic  1.43 us (1%)
    all_gather x1, blocking collectives, shards(): lax.all_gather(flat, 'col', axis=0, tiled=True, axis_index_groups=along_z)  31.8 us
    all_to_all x1, waiting for transfers between devices, shards(): whole = lax.all_to_all(sent, 'col', 0, 0, axis_index_groups=along_y)  17.5 us
    all_to_all x1, starting transfers between devices, shards(): cut = lax.all_to_all(picked.reshape(nrow, nloc // nrow, wide), 'row', 0, 0)  14 us
    slice x3, local copies, waits for them, and re-layouts, factor(): v[:, :, 1].reshape(nloc, -1)  9.22 us
    unnamed x16, local copies, waits for them, and re-layouts  4.92 us
    all_to_all x1, starting transfers between devices, shards(): lax.all_to_all(jnp.broadcast_to(cut, (nrow,) + cut.shape[1:]), 'row', 0, 0)  4.8 us
    dot_general x6, matrix products, dot(): lax.dot_general(a, b, (dims, ((), ())), preferred_element_type=jnp.float32)  4.33 us
    slice x1, local copies, waits for them, and re-layouts, factor(): v[:, :, 0].reshape(nloc, -1)  4.22 us
  transfers between devices with their start and end apart: 3, of which 2 were waited for; matrix products, arithmetic and copies ran while one was open for 20% of the time, Pallas kernels for 0%

profile of v1, /device:TPU:1, one launch (start us, length us, event | category | flops | bytes accessed | tf_op | source)
XLA Modules:
  0.0 109.6 jit_solution(1759338572207433106)
XLA Ops:
  0.6 0.8 copy.15
  1.4 0.1 iota_compare_fusion.2
  1.5 0.8 broadcast_select_fusion
  2.3 31.8 %all_gather.3 = bf16[128,2048]{1,0:T(8,128)(2,1)S(1)} all-gather(bf16[8,2048]{1,0:T(8,128)(2,1)S(1)} %broadcast_select_fusion), channel_id=1, replica_groups={{0,1,2,3,4,5,6,7,8,9,10,11,12,13,14,15},{16,17,18,19,20,21,22,23,24,25,..., dimensions={0}, use_global_device_ids=true | all-gather | bytes 557056 | tf_op jit(solution)/shard_map/all_gather | solution.py:25
  34.1 1.6 %broadcast_in_dim.45 = bf16[4,128,2048]{2,1,0:T(8,128)(2,1)} broadcast(bf16[128,2048]{1,0:T(8,128)(2,1)S(1)} %all_gather.3), dimensions={1,2} | broadcast | bytes 2621440 | tf_op jit(solution)/shard_map/broadcast_in_dim | solution.py:26
  35.6 4.2 %all-to-all-start = ((bf16[4,128,2048]{2,1,0:T(8,128)(2,1)}), bf16[4,128,2048]{2,1,0:T(8,128)(2,1)S(1)}, u32[]{:S(2)}, u32[]{:S(2)}) async-start(bf16[4,128,2048]{2,1,0:T(8,128)(2,1)} %broadcast_in_dim.45), calls=%async_computation | async-start | bytes 4194304 | tf_op jit(solution)/shard_map/all_to_all | solution.py:27
  39.8 17.5 %all-to-all-done = bf16[4,128,2048]{2,1,0:T(8,128)(2,1)S(1)} async-done(((bf16[4,128,2048]{2,1,0:T(8,128)(2,1)}), bf16[4,128,2048]{2,1,0:T(8,128)(2,1)S(1)}, u32[]{:S(2)}, u32[]{:S(2)}) %all-to-all-start) | async-done | bytes 2097184 | tf_op jit(solution)/shard_map/all_to_all | solution.py:27
  57.4 0.0 copy-start
  57.4 0.8 constant_dynamic-slice_fusion
  58.2 0.6 copy-done
  58.8 14.0 %all-to-all-start.1 = ((bf16[8,64,256]{2,1,0:T(8,128)(2,1)}), bf16[8,64,256]{2,1,0:T(8,128)(2,1)S(1)}, u32[]{:S(2)}, u32[]{:S(2)}) async-start(bf16[8,64,256]{2,1,0:T(8,128)(2,1)} %bitcast.16), calls=%async_computation.1 | async-start | bytes 524288 | tf_op jit(solution)/shard_map/all_to_all | solution.py:32
  72.8 3.2 %reshape_reshape.6 = bf16[512,8,2,128]{3,2,1,0:T(2,128)(2,1)S(1)} reshape(bf16[4,128,2048]{2,1,0:T(8,128)(2,1)} %copy-done) | data formatting | bytes 4194304 | tf_op jit(solution)/shard_map/reshape;reshape | solution.py:38
  76.0 4.2 %fusion.22 = (bf16[512,8,1,128]{3,2,1,0:T(2,128)(2,1)}, bf16[512,8,1,128]{3,2,1,0:T(2,128)(2,1)}) fusion(bf16[512,8,2,128]{3,2,1,0:T(2,128)(2,1)S(1)} %reshape_reshape.6), kind=kLoop, calls=%fused_computation.37 | loop fusion | bytes 4194304 | tf_op jit(solution)/shard_map/slice | solution.py:40
  80.2 0.0 copy-start.1
  80.2 4.7 %copy.17 = bf16[512,8,1,128]{0,3,1,2:T(8,128)(2,1)S(1)} copy(bf16[512,8,1,128]{3,2,1,0:T(2,128)(2,1)} %get-tuple-element.8) | data formatting | bytes 2097152 | tf_op jit(solution)/shard_map/slice | solution.py:40
  84.9 0.0 copy-done.1
  84.9 4.2 %copy.16 = bf16[512,8,1,128]{0,3,1,2:T(8,128)(2,1)} copy(bf16[512,8,1,128]{3,2,1,0:T(2,128)(2,1)S(1)} %copy-done.1) | data formatting | bytes 2097152 | tf_op jit(solution)/shard_map/slice | solution.py:39
  89.1 0.0 copy-start.4
  89.1 0.0 copy-start.5
  89.1 1.9 %convolution_convert_fusion = bf16[1024,512]{1,0:T(8,128)(2,1)S(1)} fusion(bf16[512,1024]{0,1:T(8,128)(2,1)S(1)} %bitcast.72, bf16[3,512,512]{2,1,0:T(8,128)(2,1)} %param.3), kind=kOutput, calls=%fused_computation.4 | convolution fusion | flops 537395200 | bytes 2621440 | tf_op jit(solution)/shard_map/dot_general | solution.py:11
  91.1 0.0 copy-done.4
  91.1 0.0 copy-done.5
  91.1 0.7 convolution_convert_fusion.2
  91.8 0.7 convolution_convert_fusion.1
  92.6 0.0 all-to-all-done.1
  92.6 0.7 broadcast_in_dim.48
  93.3 4.8 %all-to-all-start.2 = ((bf16[8,64,256]{2,1,0:T(8,128)(2,1)}), bf16[8,64,256]{2,1,0:T(8,128)(2,1)S(1)}, u32[]{:S(2)}, u32[]{:S(2)}) async-start(bf16[8,64,256]{2,1,0:T(8,128)(2,1)} %broadcast_in_dim.48), calls=%async_computation.2 | async-start | bytes 524288 | tf_op jit(solution)/shard_map/all_to_all | solution.py:34
  98.1 0.5 fusion.1
  98.7 0.6 copy.18
  99.3 0.0 copy-start.2
  99.3 0.0 copy-start.6
  99.3 1.9 %copy-done.2 = bf16[1024,8,2,128]{0,3,2,1:T(8,128)(2,1)} copy-done((bf16[1024,8,2,128]{0,3,2,1:T(8,128)(2,1)}, bf16[1024,8,2,128]{0,3,2,1:T(8,128)(2,1)S(1)}, u32[]{:S(2)}) %copy-start.2) | copy-done | bytes 4194328
  101.3 0.2 dynamic-slice_bitcast_fusion
  101.5 0.8 copy.20
  102.3 2.4 %all-to-all-done.2 = bf16[8,64,256]{2,1,0:T(8,128)(2,1)S(1)} async-done(((bf16[8,64,256]{2,1,0:T(8,128)(2,1)}), bf16[8,64,256]{2,1,0:T(8,128)(2,1)S(1)}, u32[]{:S(2)}, u32[]{:S(2)}) %all-to-all-start.2) | async-done | bytes 262176 | tf_op jit(solution)/shard_map/all_to_all | solution.py:34
  104.6 0.1 reshape_reshape.7
  104.7 0.0 copy-start.3
  104.7 0.4 fusion.23
  105.1 0.0 copy-done.6
  105.1 0.3 fusion.3
  105.4 0.3 convolution_convert_fusion.5
  105.8 0.3 fusion.2
  106.1 0.8 copy-done.3
  106.9 2.7 %select_bitcast_fusion = f32[8,1,256,256]{3,2,1,0:T(8,128)} fusion(bf16[1024,8,256]{0,2,1:T(8,128)(2,1)S(1)} %bitcast.68, bf16[1024,256,1]{0,1,2:T(8,128)(2,1)S(1)} %bitcast.74, pred[8]{0:T(512)(128)(4,1)S(1)} %add_compare_fusion), kind=kOutput, calls=%fused_computation.3 | convolution fusion | flops 1074266112 | bytes 6815752 | tf_op jit(solution)/shard_map/ktr,ks->trs/dot_general | solution.py:51
  (4 shorter events, 0.1 us)
Async XLA Ops:
  35.6 21.7 %all-to-all-start = ((bf16[4,128,2048]{2,1,0:T(8,128)(2,1)}), bf16[4,128,2048]{2,1,0:T(8,128)(2,1)S(1)}, u32[]{:S(2)}, u32[]{:S(2)}) async-start(bf16[4,128,2048]{2,1,0:T(8,128)(2,1)} %broadcast_in_dim.45), calls=%async_computation | async-start | bytes 4194304 | tf_op jit(solution)/shard_map/all_to_all | solution.py:27
  57.4 1.4 %copy-start = (bf16[4,128,2048]{2,1,0:T(8,128)(2,1)}, bf16[4,128,2048]{2,1,0:T(8,128)(2,1)S(1)}, u32[]{:S(2)}) copy-start(bf16[4,128,2048]{2,1,0:T(8,128)(2,1)S(1)} %all-to-all-done) | copy-start | bytes 6291460
  58.8 33.8 %all-to-all-start.1 = ((bf16[8,64,256]{2,1,0:T(8,128)(2,1)}), bf16[8,64,256]{2,1,0:T(8,128)(2,1)S(1)}, u32[]{:S(2)}, u32[]{:S(2)}) async-start(bf16[8,64,256]{2,1,0:T(8,128)(2,1)} %bitcast.16), calls=%async_computation.1 | async-start | bytes 524288 | tf_op jit(solution)/shard_map/all_to_all | solution.py:32
  80.2 4.7 %copy-start.1 = (bf16[512,8,1,128]{3,2,1,0:T(2,128)(2,1)S(1)}, bf16[512,8,1,128]{3,2,1,0:T(2,128)(2,1)}, u32[]{:S(2)}) copy-start(bf16[512,8,1,128]{3,2,1,0:T(2,128)(2,1)} %get-tuple-element.9) | copy-start | bytes 3145732
  89.1 1.9 %copy-start.4 = (bf16[512,8,1,128]{0,3,1,2:T(8,128)(2,1)S(1)}, bf16[512,8,1,128]{0,3,1,2:T(8,128)(2,1)}, u32[]{:S(2)}) copy-start(bf16[512,8,1,128]{0,3,1,2:T(8,128)(2,1)} %copy.16) | copy-start | bytes 3145732
  89.1 1.9 %copy-start.5 = (bf16[3,512,512]{2,1,0:T(8,128)(2,1)S(1)}, bf16[3,512,512]{2,1,0:T(8,128)(2,1)}, u32[]{:S(2)}) copy-start(bf16[3,512,512]{2,1,0:T(8,128)(2,1)} %param.3) | copy-start | bytes 4718596
  93.3 11.3 %all-to-all-start.2 = ((bf16[8,64,256]{2,1,0:T(8,128)(2,1)}), bf16[8,64,256]{2,1,0:T(8,128)(2,1)S(1)}, u32[]{:S(2)}, u32[]{:S(2)}) async-start(bf16[8,64,256]{2,1,0:T(8,128)(2,1)} %broadcast_in_dim.48), calls=%async_computation.2 | async-start | bytes 524288 | tf_op jit(solution)/shard_map/all_to_all | solution.py:34
  99.3 2.0 %copy-start.2 = (bf16[1024,8,2,128]{0,3,2,1:T(8,128)(2,1)}, bf16[1024,8,2,128]{0,3,2,1:T(8,128)(2,1)S(1)}, u32[]{:S(2)}) copy-start(bf16[1024,8,2,128]{0,3,2,1:T(8,128)(2,1)S(1)} %copy.18) | copy-start | bytes 12582916
  99.3 5.8 %copy-start.6 = (bf16[3,512,512]{2,1,0:T(8,128)(2,1)S(1)}, bf16[3,512,512]{2,1,0:T(8,128)(2,1)}, u32[]{:S(2)}) copy-start(bf16[3,512,512]{2,1,0:T(8,128)(2,1)} %param.3) | copy-start | bytes 4718596
  104.7 2.2 %copy-start.3 = (bf16[1024,8,2,128]{0,3,2,1:T(8,128)(2,1)S(1)}, bf16[1024,8,2,128]{0,3,2,1:T(8,128)(2,1)}, u32[]{:S(2)}) copy-start(bf16[1024,8,2,128]{0,3,2,1:T(8,128)(2,1)} %copy-done.2) | copy-start | bytes 12582916

commit v2 on v1

v2 whole, which is shorter than its diff:
```python
import jax
import jax.numpy as jnp
from jax import lax
from jax.experimental import pallas as pl
from jax.experimental.pallas import tpu as pltpu
from jax.sharding import PartitionSpec as P

Y = 4
Z = 16
BF16 = jnp.bfloat16


def dot(a, b, ca, cb):
    return lax.dot_general(a, b, (((ca,), (cb,)), ((), ())), preferred_element_type=jnp.float32)


def own_factors(place, ranks, diag, v, wt, lt, rt, share):
    step = pl.program_id(0)
    piece = share.shape[1]
    nloc = v.shape[0]
    rank = v.shape[1] // 4
    q = place[0]
    half = nloc // piece
    rows = pl.ds(pl.multiple_of(lax.rem(q, half) * piece, piece), piece)
    first = q < half
    row = lax.broadcasted_iota(jnp.int32, (2 * rank, 1), 0)
    lane = lax.broadcasted_iota(jnp.int32, (1, 2 * rank), 1)

    def keep(at, k):
        one, two = ranks[4 * step + k], ranks[4 * step + 2 + k]
        return at < jnp.where(at < rank, one, two + rank)

    block = v[...]
    v0 = jnp.concatenate([block[:, :rank], block[:, 2 * rank : 3 * rank]], 1)
    v1 = jnp.concatenate([block[:, rank : 2 * rank], block[:, 3 * rank :]], 1)
    w = dot(v0, diag[0], 0, 1)
    w = jnp.where(keep(row, 0), w, 0.0).astype(BF16)
    wt[...] = w
    lt[...] = dot(w, diag[1], 1, 1).astype(BF16)
    r = dot(v1, diag[2], 0, 1)
    rt[...] = jnp.where(keep(row, 1), r, 0.0).astype(BF16)
    top = jnp.where(keep(lane, 0), dot(diag[0, rows, :], v0, 1, 0), 0.0)
    low = dot(diag[1, rows, :], w, 1, 1)
    side = jnp.where(keep(lane, 1), dot(diag[2, rows, :], v1, 1, 0), 0.0)
    left = jnp.where(first, top, low).astype(BF16)
    right = jnp.where(first, 0.0, side).astype(BF16)
    for t in range(2):
        cut = slice(t * rank, (t + 1) * rank)
        share[t, :, :rank] = left[:, cut]
        share[t, :, rank:] = right[:, cut]


def tile_cores(place, diag, column, wt, lt, rt, cores, wc, lrc):
    step = pl.program_id(0)
    rank = wc.shape[1]

    @pl.when(step == 0)
    def _():
        w = dot(diag[0], column[:, :rank], 1, 0).astype(BF16)
        wc[...] = w
        lrc[:, :rank] = dot(diag[1], w, 1, 0).astype(BF16)
        lrc[:, rank:] = dot(diag[2], column[:, rank:], 1, 0).astype(BF16)

    both = dot(lt[...], lrc[...], 1, 0)
    corner = dot(wt[...], wc[...], 1, 0)
    below = dot(rt[...], lrc[...], 1, 0)
    for t in range(2):
        cut = slice(t * rank, (t + 1) * rank)
        active = (2 * step + t) * place[2] + place[1] > place[0]
        cores[t, :rank, :rank] = jnp.where(active, both[cut, :rank] + corner[cut], 0.0)
        cores[t, :rank, rank:] = jnp.where(active, both[cut, rank:], 0.0)
        cores[t, rank:, :] = jnp.where(active, below[cut], 0.0)


def shards(diag_factors, panel_v, ranks):
    tiles, pair, mine, rank = panel_v.shape
    nrow = lax.axis_size("row")
    ncol = lax.axis_size("col")
    prow = lax.axis_index("row")
    qcol = lax.axis_index("col")
    along_z = [[y * Z + z for z in range(Z)] for y in range(Y)]
    along_y = [[y * Z + z for y in range(Y)] for z in range(Z)]
    wide = pair * rank
    place = jnp.stack([qcol, prow, jnp.int32(nrow)]).astype(jnp.int32)
    flat = panel_v.transpose(2, 0, 1, 3).reshape(mine, tiles * wide)
    slab = lax.all_gather(flat, "col", axis=0, tiled=True, axis_index_groups=along_z)
    sent = jnp.broadcast_to(slab[None], (Y,) + slab.shape)
    whole = lax.all_to_all(sent, "col", 0, 0, axis_index_groups=along_y)
    whole = whole.reshape(-1, flat.shape[1])
    nloc = whole.shape[0]
    local_row = qcol // nrow
    picked = lax.dynamic_slice_in_dim(whole, local_row * wide, wide, 1)
    limit = lax.dynamic_index_in_dim(ranks, local_row, 0, keepdims=False)
    at = jnp.arange(wide, dtype=jnp.int32)
    keep = jnp.where(at < rank, at < limit[0], at < limit[1] + rank)
    picked = jnp.where(keep[None], picked, jnp.zeros_like(picked))
    cut = lax.all_to_all(picked.reshape(nrow, nloc // nrow, wide), "row", 0, 0)
    cut = lax.dynamic_index_in_dim(cut, qcol % nrow, 0, keepdims=True)
    column = lax.all_to_all(jnp.broadcast_to(cut, (nrow,) + cut.shape[1:]), "row", 0, 0)
    column = column.reshape(nloc, wide)

    steps = tiles // 2
    scalars = pl.BlockSpec(memory_space=pltpu.SMEM)
    matrices = pl.BlockSpec(diag_factors.shape, lambda i: (0, 0, 0))
    turned = pl.BlockSpec((wide, nloc), lambda i: (i, 0))
    lying = jax.ShapeDtypeStruct((tiles * rank, nloc), BF16)
    piece = 2 * nloc // ncol
    limits = pltpu.CompilerParams(vmem_limit_bytes=32 << 20)
    wt, lt, rt, share = pl.pallas_call(
        own_factors,
        grid=(steps,),
        in_specs=[scalars, scalars, matrices, pl.BlockSpec((nloc, 2 * wide), lambda i: (0, i))],
        out_specs=[turned] * 3 + [pl.BlockSpec((2, piece, wide), lambda i: (i, 0, 0))],
        out_shape=[lying] * 3 + [jax.ShapeDtypeStruct((tiles, piece, wide), BF16)],
        compiler_params=limits,
        cost_estimate=pl.CostEstimate(flops=8 * 10**9, bytes_accessed=8 << 20, transcendentals=0),
        name="own_factors",
    )(place, ranks.reshape(-1), diag_factors, whole)
    cores = pl.pallas_call(
        tile_cores,
        grid=(steps,),
        in_specs=[scalars, matrices, pl.BlockSpec((nloc, wide), lambda i: (0, 0))] + [turned] * 3,
        out_specs=pl.BlockSpec((2, wide, wide), lambda i: (i, 0, 0)),
        out_shape=jax.ShapeDtypeStruct((tiles, wide, wide), jnp.float32),
        scratch_shapes=[pltpu.VMEM((nloc, rank), BF16), pltpu.VMEM((nloc, wide), BF16)],
        compiler_params=limits,
        cost_estimate=pl.CostEstimate(flops=2 * 10**9, bytes_accessed=7 << 20, transcendentals=0),
        name="tile_cores",
    )(place, diag_factors, column, wt, lt, rt)
    return share, cores[:, None]


def solution(mesh):
    placed = (P(), P("row", None, "col", None), P("row", None))
    return jax.shard_map(
        shards,
        mesh=mesh,
        in_specs=placed,
        out_specs=(P("row", "col", None), P("row", "col", None, None)),
        check_vma=False,
    )
```

time: 110 us -> 98.7 us (0.90)
  local copies, waits for them, and re-layouts: 25.6 us -> 10.4 us
  Pallas kernels: 0 us -> 8.35 us
  matrix products: 6.99 us -> 0 us
  waiting for transfers between devices: 19.9 us -> 21.9 us
    slice x4 -> x1, local copies, waits for them, and re-layouts: 13.4 us -> 0.58 us  [shards(): keep = jnp.where(at < rank, at < limit[0], at < limit[1] + rank)]
    pallas_call x0 -> x2, Pallas kernels: none -> 8.35 us  [the longest x1 4.48 us: shards(): pl.pallas_call(own_factors, grid=(steps,), in_specs=[scalars, scalars, ma...]
    dot_general x7 -> x0, matrix products: 6.99 us -> none  [the longest x6 4.33 us: dot(): lax.dot_general(a, b, (dims, ((), ())), preferred_element_type=jnp.float32)]
    all_to_all x1, waiting for transfers between devices: 0.01 us -> 6.26 us  [shards(): cut = lax.all_to_all(picked.reshape(nrow, nloc // nrow, wide), 'row', 0, 0)]
    another operation x2 -> x0, local copies, waits for them, and re-layouts: 3.29 us -> none  [factor(): v = v.reshape(nloc, -1, pair, rank)]
    unnamed x16 -> x15, local copies, waits for them, and re-layouts: 4.92 us -> 7.3 us
    all_to_all x1, waiting for transfers between devices: 2.35 us -> 0.01 us  [shards(): lax.all_to_all(jnp.broadcast_to(cut, (nrow,) + cut.shape[1:]), 'row', 0, 0)]
    all_to_all x1, waiting for transfers between devices: 17.5 us -> 15.6 us  [shards(): whole = lax.all_to_all(sent, 'col', 0, 0, axis_index_groups=along_y)]
  transfers between devices with their start and end apart: 3 -> 3, of which waited for: 2 -> 2; matrix products, arithmetic and copies ran while one was open for 20% -> 2% of each run, Pallas kernels for 0% -> 5%
where the time goes in v2:
time: 98.7 us; the launch traced here: 98.1 us
  blocking collectives  32.1 us (33%)
  starting transfers between devices  22.7 us (23%)
  waiting for transfers between devices  21.9 us (22%)
  local copies, waits for them, and re-layouts  10.4 us (11%)
  Pallas kernels  8.35 us (8%)
  other arithmetic  1.49 us (2%)
  between operations  1.28 us (1%)
    all_gather x1, blocking collectives, shards(): lax.all_gather(flat, 'col', axis=0, tiled=True, axis_index_groups=along_z)  32.1 us
    all_to_all x1, waiting for transfers between devices, shards(): whole = lax.all_to_all(sent, 'col', 0, 0, axis_index_groups=along_y)  15.6 us
    all_to_all x1, starting transfers between devices, shards(): cut = lax.all_to_all(picked.reshape(nrow, nloc // nrow, wide), 'row', 0, 0)  14 us
    unnamed x15, local copies, waits for them, and re-layouts  7.3 us
    all_to_all x1, waiting for transfers between devices, shards(): cut = lax.all_to_all(picked.reshape(nrow, nloc // nrow, wide), 'row', 0, 0)  6.26 us
    pallas_call x1, Pallas kernels, shards(): pl.pallas_call(own_factors, grid=(steps,), in_specs=[scalars, scalars, ma...  4.48 us
    all_to_all x1, starting transfers between devices, shards(): lax.all_to_all(jnp.broadcast_to(cut, (nrow,) + cut.shape[1:]), 'row', 0, 0)  4.35 us
    all_to_all x1, starting transfers between devices, shards(): whole = lax.all_to_all(sent, 'col', 0, 0, axis_index_groups=along_y)  4.31 us
  transfers between devices with their start and end apart: 3, of which 2 were waited for; matrix products, arithmetic and copies ran while one was open for 2% of the time, Pallas kernels for 5%

profile of v2, /device:TPU:1, one launch (start us, length us, event | category | flops | bytes accessed | tf_op | source)
XLA Modules:
  0.0 98.1 jit_solution(11000148841595136290)
XLA Ops:
  0.6 32.1 %all_gather.3 = bf16[128,2048]{1,0:T(8,128)(2,1)S(1)} all-gather(bf16[8,2048]{1,0:T(8,128)(2,1)} %bitcast.18), channel_id=1, replica_groups={{0,1,2,3,4,5,6,7,8,9,10,11,12,13,14,15},{16,17,18,19,20,21,22,23,24,25,..., dimensions={0}, use_global_device_ids=true | all-gather | bytes 557056 | tf_op jit(solution)/shard_map/all_gather | solution.py:86
  32.7 1.6 %broadcast_in_dim.28 = bf16[4,128,2048]{2,1,0:T(8,128)(2,1)} broadcast(bf16[128,2048]{1,0:T(8,128)(2,1)S(1)} %all_gather.3), dimensions={1,2} | broadcast | bytes 2621440 | tf_op jit(solution)/shard_map/broadcast_in_dim | solution.py:87
  34.3 0.0 copy-start.6
  34.3 4.3 %all-to-all-start = ((bf16[4,128,2048]{2,1,0:T(8,128)(2,1)}), bf16[4,128,2048]{2,1,0:T(8,128)(2,1)S(1)}, u32[]{:S(2)}, u32[]{:S(2)}) async-start(bf16[4,128,2048]{2,1,0:T(8,128)(2,1)} %broadcast_in_dim.28), calls=%async_computation | async-start | bytes 4194304 | tf_op jit(solution)/shard_map/all_to_all | solution.py:88
  38.6 0.0 copy-done.6
  38.6 0.1 constant_dynamic-slice_fusion
  38.7 0.6 fusion
  39.9 0.7 compare_select_fusion
  40.5 15.6 %all-to-all-done = bf16[4,128,2048]{2,1,0:T(8,128)(2,1)S(1)} async-done(((bf16[4,128,2048]{2,1,0:T(8,128)(2,1)}), bf16[4,128,2048]{2,1,0:T(8,128)(2,1)S(1)}, u32[]{:S(2)}, u32[]{:S(2)}) %all-to-all-start) | async-done | bytes 2097184 | tf_op jit(solution)/shard_map/all_to_all | solution.py:88
  56.1 0.8 dynamic-slice_select_fusion
  56.9 14.0 %all-to-all-start.1 = ((bf16[8,64,256]{2,1,0:T(8,128)(2,1)}), bf16[8,64,256]{2,1,0:T(8,128)(2,1)S(1)}, u32[]{:S(2)}, u32[]{:S(2)}) async-start(bf16[8,64,256]{2,1,0:T(8,128)(2,1)} %bitcast.7), calls=%async_computation.1 | async-start | bytes 524288 | tf_op jit(solution)/shard_map/all_to_all | solution.py:97
  70.9 0.1 copy.7
  71.0 0.1 reshape.35.ranks
  71.1 0.1 pad_add_fusion.place
  71.2 6.3 %all-to-all-done.1 = bf16[8,64,256]{2,1,0:T(8,128)(2,1)S(1)} async-done(((bf16[8,64,256]{2,1,0:T(8,128)(2,1)}), bf16[8,64,256]{2,1,0:T(8,128)(2,1)S(1)}, u32[]{:S(2)}, u32[]{:S(2)}) %all-to-all-start.1) | async-done | bytes 262176 | tf_op jit(solution)/shard_map/all_to_all | solution.py:97
  77.4 0.7 broadcast_in_dim.32
  78.2 4.4 %all-to-all-start.2 = ((bf16[8,64,256]{2,1,0:T(8,128)(2,1)}), bf16[8,64,256]{2,1,0:T(8,128)(2,1)S(1)}, u32[]{:S(2)}, u32[]{:S(2)}) async-start(bf16[8,64,256]{2,1,0:T(8,128)(2,1)} %broadcast_in_dim.32), calls=%async_computation.2 | async-start | bytes 524288 | tf_op jit(solution)/shard_map/all_to_all | solution.py:99
  82.5 0.0 copy-start
  82.5 1.4 %copy-done = bf16[3,512,512]{2,1,0:T(8,128)(2,1)S(1)} copy-done((bf16[3,512,512]{2,1,0:T(8,128)(2,1)S(1)}, bf16[3,512,512]{2,1,0:T(8,128)(2,1)}, u32[]{:S(2)}) %copy-start) | copy-done | bytes 1572888
  83.9 4.5 %own_factors.1 = (bf16[1024,512]{1,0:T(8,128)(2,1)S(1)}, bf16[1024,512]{1,0:T(8,128)(2,1)S(1)}, bf16[1024,512]{1,0:T(8,128)(2,1)S(1)}, bf16[8,16,256]{2,1,0:T(8,128)(2,1)}) custom-call(s32[3]{0:T(128)S(1)} %pad_add_fusion.place, s32[16]{0:T(128)S(1)} %reshape.35.ranks, bf16[3,512,512]{2,1,0:T(8,128)(2,1)S(1)} %copy-done, bf16[512,2048]{1,0:T(8,128)(2,1)S(1)} %bitcast.16), custom_call_target="tpu_custom_call" | custom-call | flops 8000000000 | bytes 8388608 | tf_op jit(solution)/shard_map/own_factors/pallas_call | solution.py:109
  88.4 0.0 copy-start.2
  88.4 1.0 copy-done.2
  89.4 0.0 copy-start.4
  89.4 1.0 copy-done.4
  90.4 0.0 all-to-all-done.2
  90.4 0.0 copy-start.1
  90.4 1.4 %copy-done.1 = bf16[3,512,512]{2,1,0:T(8,128)(2,1)S(1)} copy-done((bf16[3,512,512]{2,1,0:T(8,128)(2,1)S(1)}, bf16[3,512,512]{2,1,0:T(8,128)(2,1)}, u32[]{:S(2)}) %copy-start.1) | copy-done | bytes 1572888
  91.8 0.0 copy-start.3
  91.8 1.2 %copy-done.3 = bf16[1024,512]{1,0:T(8,128)(2,1)S(1)} copy-done((bf16[1024,512]{1,0:T(8,128)(2,1)S(1)}, bf16[1024,512]{1,0:T(8,128)(2,1)}, u32[]{:S(2)}) %copy-start.3) | copy-done | bytes 1048600
  93.0 0.0 copy-start.5
  93.0 1.2 %copy-done.5 = bf16[1024,512]{1,0:T(8,128)(2,1)S(1)} copy-done((bf16[1024,512]{1,0:T(8,128)(2,1)S(1)}, bf16[1024,512]{1,0:T(8,128)(2,1)}, u32[]{:S(2)}) %copy-start.5) | copy-done | bytes 1048600
  94.2 3.9 %tile_cores.1 = f32[8,256,256]{2,1,0:T(8,128)} custom-call(s32[3]{0:T(128)S(1)} %pad_add_fusion.place, bf16[3,512,512]{2,1,0:T(8,128)(2,1)S(1)} %copy-done.1, bf16[512,256]{1,0:T(8,128)(2,1)S(1)} %bitcast.17, bf16[1024,512]{1,0:T(8,128)(2,1)S(1)} %get-tuple-element.7.wt, bf16[1024,512]{1,0:T(8,128)(2,1)S(1)} %copy-done.3, bf16[1024,512]{1,0:T(8,128)(2,1)S(1)} %copy-done.5), custom_call_target="tpu_custom_call" | custom-call | flops 2000000000 | bytes 7340032 | tf_op jit(solution)/shard_map/tile_cores/pallas_call | solution.py:119
  (1 shorter events, 0.0 us)
Async XLA Ops:
  34.3 4.3 %copy-start.6 = (s32[8,2]{0,1:T(2,128)S(1)}, s32[8,2]{0,1:T(2,128)}, u32[]{:S(2)}) copy-start(s32[8,2]{0,1:T(2,128)} %param.5) | copy-start | bytes 196
  34.3 21.9 %all-to-all-start = ((bf16[4,128,2048]{2,1,0:T(8,128)(2,1)}), bf16[4,128,2048]{2,1,0:T(8,128)(2,1)S(1)}, u32[]{:S(2)}, u32[]{:S(2)}) async-start(bf16[4,128,2048]{2,1,0:T(8,128)(2,1)} %broadcast_in_dim.28), calls=%async_computation | async-start | bytes 4194304 | tf_op jit(solution)/shard_map/all_to_all | solution.py:88
  56.9 20.5 %all-to-all-start.1 = ((bf16[8,64,256]{2,1,0:T(8,128)(2,1)}), bf16[8,64,256]{2,1,0:T(8,128)(2,1)S(1)}, u32[]{:S(2)}, u32[]{:S(2)}) async-start(bf16[8,64,256]{2,1,0:T(8,128)(2,1)} %bitcast.7), calls=%async_computation.1 | async-start | bytes 524288 | tf_op jit(solution)/shard_map/all_to_all | solution.py:97
  78.2 12.2 %all-to-all-start.2 = ((bf16[8,64,256]{2,1,0:T(8,128)(2,1)}), bf16[8,64,256]{2,1,0:T(8,128)(2,1)S(1)}, u32[]{:S(2)}, u32[]{:S(2)}) async-start(bf16[8,64,256]{2,1,0:T(8,128)(2,1)} %broadcast_in_dim.32), calls=%async_computation.2 | async-start | bytes 524288 | tf_op jit(solution)/shard_map/all_to_all | solution.py:99
  82.5 1.4 %copy-start = (bf16[3,512,512]{2,1,0:T(8,128)(2,1)S(1)}, bf16[3,512,512]{2,1,0:T(8,128)(2,1)}, u32[]{:S(2)}) copy-start(bf16[3,512,512]{2,1,0:T(8,128)(2,1)} %diag.3) | copy-start | bytes 4718596
  88.4 1.0 copy-start.2
  89.4 1.0 %copy-start.4 = (bf16[1024,512]{1,0:T(8,128)(2,1)}, bf16[1024,512]{1,0:T(8,128)(2,1)S(1)}, u32[]{:S(2)}) copy-start(bf16[1024,512]{1,0:T(8,128)(2,1)S(1)} %get-tuple-element.9.rt) | copy-start | bytes 3145732
  90.4 1.4 %copy-start.1 = (bf16[3,512,512]{2,1,0:T(8,128)(2,1)S(1)}, bf16[3,512,512]{2,1,0:T(8,128)(2,1)}, u32[]{:S(2)}) copy-start(bf16[3,512,512]{2,1,0:T(8,128)(2,1)} %diag.3) | copy-start | bytes 4718596
  91.8 1.2 %copy-start.3 = (bf16[1024,512]{1,0:T(8,128)(2,1)S(1)}, bf16[1024,512]{1,0:T(8,128)(2,1)}, u32[]{:S(2)}) copy-start(bf16[1024,512]{1,0:T(8,128)(2,1)} %copy-done.2) | copy-start | bytes 3145732
  93.0 1.2 %copy-start.5 = (bf16[1024,512]{1,0:T(8,128)(2,1)S(1)}, bf16[1024,512]{1,0:T(8,128)(2,1)}, u32[]{:S(2)}) copy-start(bf16[1024,512]{1,0:T(8,128)(2,1)} %copy-done.4) | copy-start | bytes 3145732

commit v3 on v2

v3 whole, which is shorter than its diff:
```python
import jax
import jax.numpy as jnp
from jax import lax
from jax.experimental import pallas as pl
from jax.experimental.pallas import tpu as pltpu
from jax.sharding import PartitionSpec as P

Y = 4
Z = 16
BF16 = jnp.bfloat16


def dot(a, b, ca, cb):
    return lax.dot_general(a, b, (((ca,), (cb,)), ((), ())), preferred_element_type=jnp.float32)


def pick_tiles(place, ranks, ta, tb, tc, td, picked):
    rank = picked.shape[3] // 2
    lane = lax.broadcasted_iota(jnp.int32, (1, 2 * rank), 1)
    for y, tile in enumerate((ta, tb, tc, td)):
        at = place[4 + y]
        keep = lane < jnp.where(lane < rank, ranks[0, at], ranks[1, at] + rank)
        kept = jnp.where(keep, tile[...].astype(jnp.float32), 0.0).astype(BF16)
        picked[:, y] = kept.reshape(picked.shape[0], picked.shape[2], picked.shape[3])


def own_factors(place, ranks, diag, va, vb, vc, vd, wt, lt, rt, share, block):
    step = pl.program_id(0)
    piece = share.shape[1]
    nloc, rank = block.shape[0], block.shape[1] // 4
    part = nloc // Y
    q = place[0]
    half = nloc // piece
    rows = pl.ds(pl.multiple_of(lax.rem(q, half) * piece, piece), piece)
    first = q < half
    row = lax.broadcasted_iota(jnp.int32, (2 * rank, 1), 0)
    lane = lax.broadcasted_iota(jnp.int32, (1, 2 * rank), 1)

    def keep(at, k):
        one, two = ranks[k, 2 * step], ranks[k, 2 * step + 1]
        return at < jnp.where(at < rank, one, two + rank)

    for d, v in enumerate((va, vb, vc, vd)):
        source = lax.rem(place[3] + Y - d, Y)
        block[pl.ds(pl.multiple_of(source * part, part), part), :] = v[...]
    v0 = jnp.concatenate([block[:, :rank], block[:, 2 * rank : 3 * rank]], 1)
    v1 = jnp.concatenate([block[:, rank : 2 * rank], block[:, 3 * rank :]], 1)
    w = dot(v0, diag[0], 0, 1)
    w = jnp.where(keep(row, 0), w, 0.0).astype(BF16)
    wt[...] = w
    lt[...] = dot(w, diag[1], 1, 1).astype(BF16)
    r = dot(v1, diag[2], 0, 1)
    rt[...] = jnp.where(keep(row, 1), r, 0.0).astype(BF16)
    top = jnp.where(keep(lane, 0), dot(diag[0, rows, :], v0, 1, 0), 0.0)
    low = dot(diag[1, rows, :], w, 1, 1)
    side = jnp.where(keep(lane, 1), dot(diag[2, rows, :], v1, 1, 0), 0.0)
    left = jnp.where(first, top, low).astype(BF16)
    right = jnp.where(first, 0.0, side).astype(BF16)
    for t in range(2):
        cut = slice(t * rank, (t + 1) * rank)
        share[t, :, :rank] = left[:, cut]
        share[t, :, rank:] = right[:, cut]


def tile_cores(place, diag, cuts, wt, lt, rt, cores, column, wc, lrc):
    step = pl.program_id(0)
    rank = wc.shape[1]

    @pl.when(step == 0)
    def _():
        rows = cuts.shape[1] // Y
        for y in range(Y):
            for p in range(cuts.shape[0]):
                at = (y * cuts.shape[0] + p) * rows
                column[at : at + rows, :] = cuts[p, y * rows : (y + 1) * rows, :]
        w = dot(diag[0], column[:, :rank], 1, 0).astype(BF16)
        wc[...] = w
        lrc[:, :rank] = dot(diag[1], w, 1, 0).astype(BF16)
        lrc[:, rank:] = dot(diag[2], column[:, rank:], 1, 0).astype(BF16)

    both = dot(lt[...], lrc[...], 1, 0)
    corner = dot(wt[...], wc[...], 1, 0)
    below = dot(rt[...], lrc[...], 1, 0)
    for t in range(2):
        cut = slice(t * rank, (t + 1) * rank)
        active = (2 * step + t) * place[2] + place[1] > place[0]
        cores[t, :rank, :rank] = jnp.where(active, both[cut, :rank] + corner[cut], 0.0)
        cores[t, :rank, rank:] = jnp.where(active, both[cut, rank:], 0.0)
        cores[t, rank:, :] = jnp.where(active, below[cut], 0.0)


def shards(diag_factors, panel_v, ranks):
    tiles, pair, mine, rank = panel_v.shape
    nrow = lax.axis_size("row")
    ncol = lax.axis_size("col")
    prow = lax.axis_index("row")
    qcol = lax.axis_index("col")
    along_z = [[y * Z + z for z in range(Z)] for y in range(Y)]
    across = [[(p * Y + y) * Z + z for p in range(nrow) for y in range(Y)] for z in range(Z)]
    wide = pair * rank
    ycol, zcol = qcol // Z, qcol % Z
    local = [(y * Z + zcol) // nrow for y in range(Y)]
    place = jnp.stack([qcol, prow, jnp.int32(nrow), ycol] + local).astype(jnp.int32)
    flat = panel_v.transpose(2, 0, 1, 3).reshape(mine, tiles * wide)
    slab = lax.all_gather(flat, "col", axis=0, tiled=True, axis_index_groups=along_z)
    parts = [slab] + [
        lax.ppermute(slab, "col", [(y * Z + z, (y + d) % Y * Z + z) for y in range(Y) for z in range(Z)])
        for d in range(1, Y)
    ]
    nloc = Y * slab.shape[0]
    rows = slab.shape[0] // nrow

    def of(y):
        return pl.BlockSpec((slab.shape[0], wide), lambda i, where: (0, where[4 + y]))

    picked = pl.pallas_call(
        pick_tiles,
        grid_spec=pltpu.PrefetchScalarGridSpec(
            num_scalar_prefetch=1,
            grid=(1,),
            in_specs=[pl.BlockSpec(memory_space=pltpu.SMEM)] + [of(y) for y in range(Y)],
            out_specs=pl.BlockSpec((nrow, Y, rows, wide), lambda i, where: (0, 0, 0, 0)),
        ),
        out_shape=jax.ShapeDtypeStruct((nrow, Y, rows, wide), BF16),
        compiler_params=pltpu.CompilerParams(vmem_limit_bytes=4 << 20),
        name="pick_tiles",
    )(place, ranks.T, *[slab] * Y)
    picked = picked.reshape(nrow * Y, rows, wide)
    cut = lax.all_to_all(picked, ("row", "col"), 0, 0, axis_index_groups=across)
    cut = lax.dynamic_slice_in_dim(cut, zcol % nrow * Y, Y, 0).reshape(1, Y * rows, wide)
    cuts = lax.all_to_all(jnp.broadcast_to(cut, (nrow,) + cut.shape[1:]), "row", 0, 0)

    steps = tiles // 2
    scalars = pl.BlockSpec(memory_space=pltpu.SMEM)
    matrices = pl.BlockSpec(diag_factors.shape, lambda i: (0, 0, 0))
    turned = pl.BlockSpec((wide, nloc), lambda i: (i, 0))
    lying = pltpu.HBM((tiles * rank, nloc), BF16)
    piece = 2 * nloc // ncol
    limits = pltpu.CompilerParams(vmem_limit_bytes=16 << 20)
    wt, lt, rt, share = pl.pallas_call(
        own_factors,
        grid=(steps,),
        in_specs=[scalars, scalars, matrices] + [pl.BlockSpec((nloc // Y, 2 * wide), lambda i: (0, i))] * Y,
        out_specs=[turned] * 3 + [pl.BlockSpec((2, piece, wide), lambda i: (i, 0, 0))],
        out_shape=[lying] * 3 + [jax.ShapeDtypeStruct((tiles, piece, wide), BF16)],
        scratch_shapes=[pltpu.VMEM((nloc, 2 * wide), BF16)],
        compiler_params=limits,
        cost_estimate=pl.CostEstimate(flops=8 * 10**9, bytes_accessed=8 << 20, transcendentals=0),
        name="own_factors",
    )(place, ranks.T, diag_factors, *parts)
    cores = pl.pallas_call(
        tile_cores,
        grid=(steps,),
        in_specs=[scalars, matrices, pl.BlockSpec(cuts.shape, lambda i: (0, 0, 0))] + [turned] * 3,
        out_specs=pl.BlockSpec((2, wide, wide), lambda i: (i, 0, 0)),
        out_shape=jax.ShapeDtypeStruct((tiles, wide, wide), jnp.float32),
        scratch_shapes=[pltpu.VMEM((nloc, n), BF16) for n in (wide, rank, wide)],
        compiler_params=limits,
        cost_estimate=pl.CostEstimate(flops=2 * 10**9, bytes_accessed=7 << 20, transcendentals=0),
        name="tile_cores",
    )(place, diag_factors, cuts, *[pltpu.with_memory_space_constraint(a, pltpu.HBM) for a in (wt, lt, rt)])
    return share, cores[:, None]


def solution(mesh):
    placed = (P(), P("row", None, "col", None), P("row", None))
    return jax.shard_map(
        shards,
        mesh=mesh,
        in_specs=placed,
        out_specs=(P("row", "col", None), P("row", "col", None, None)),
        check_vma=False,
    )
```

time: 98.7 us -> 85.6 us (0.87)
  waiting for transfers between devices: 21.9 us -> 9.87 us
  local copies, waits for them, and re-layouts: 10.4 us -> 1.5 us
  starting transfers between devices: 22.7 us -> 28.4 us
  Pallas kernels: 8.35 us -> 12.5 us
  other arithmetic: 1.49 us -> 0 us
    all_to_all x2 -> x1, waiting for transfers between devices: 21.9 us -> 8.79 us  [shards(): cut = lax.all_to_all(picked, ('row', 'col'), 0, 0, axis_index_groups=across)]
    ppermute x0 -> x3, starting transfers between devices: none -> 10.8 us  [shards(): lax.ppermute(slab, 'col', [(y * Z + z, (y + d) % Y * Z + z) for y in rang...]
    unnamed x15 -> x6, local copies, waits for them, and re-layouts: 7.3 us -> 0.69 us
    all_to_all x2 -> x1, starting transfers between devices: 18.4 us -> 13.7 us  [shards(): cut = lax.all_to_all(picked, ('row', 'col'), 0, 0, axis_index_groups=across)]
    pallas_call x0 -> x1, Pallas kernels: none -> 1.84 us  [shards(): pl.pallas_call(pick_tiles, grid_spec=pltpu.PrefetchScalarGridSpec(num_sca...]
    broadcast_in_dim x1 -> x0, local copies, waits for them, and re-layouts: 1.58 us -> none  [shards(): sent = jnp.broadcast_to(slab[None], (Y,) + slab.shape)]
    select_n x2 -> x0, other arithmetic: 1.42 us -> none  [the longest x1 0.77 us: shards(): picked = jnp.where(keep[None], picked, jnp.zeros_like(picked))]
    pallas_call x1, Pallas kernels: 3.86 us -> 5.24 us  [shards(): pl.pallas_call(tile_cores, grid=(steps,), in_specs=[scalars, matrices, pl...]
  transfers between devices with their start and end apart: 3 -> 5, of which waited for: 2 -> 2; matrix products, arithmetic and copies ran while one was open for 2% -> 1% of each run, Pallas kernels for 5% -> 9%
where the time goes in v3:
time: 85.6 us; the launch traced here: 85.1 us
  blocking collectives  32.1 us (38%)
  starting transfers between devices  28.4 us (33%)
  Pallas kernels  12.5 us (15%)
  waiting for transfers between devices  9.87 us (12%)
  local copies, waits for them, and re-layouts  1.5 us (2%)
    all_gather x1, blocking collectives, shards(): lax.all_gather(flat, 'col', axis=0, tiled=True, axis_index_groups=along_z)  32.1 us
    all_to_all x1, starting transfers between devices, shards(): cut = lax.all_to_all(picked, ('row', 'col'), 0, 0, axis_index_groups=across)  13.7 us
    ppermute x3, starting transfers between devices, shards(): lax.ppermute(slab, 'col', [(y * Z + z, (y + d) % Y * Z + z) for y in rang...  10.8 us
    all_to_all x1, waiting for transfers between devices, shards(): cut = lax.all_to_all(picked, ('row', 'col'), 0, 0, axis_index_groups=across)  8.79 us
    pallas_call x1, Pallas kernels, shards(): pl.pallas_call(own_factors, grid=(steps,), in_specs=[scalars, scalars, ma...  5.41 us
    pallas_call x1, Pallas kernels, shards(): pl.pallas_call(tile_cores, grid=(steps,), in_specs=[scalars, matrices, pl...  5.24 us
    all_to_all x1, starting transfers between devices, shards(): lax.all_to_all(jnp.broadcast_to(cut, (nrow,) + cut.shape[1:]), 'row', 0, 0)  3.89 us
    pallas_call x1, Pallas kernels, shards(): pl.pallas_call(pick_tiles, grid_spec=pltpu.PrefetchScalarGridSpec(num_sca...  1.84 us
  transfers between devices with their start and end apart: 5, of which 2 were waited for; matrix products, arithmetic and copies ran while one was open for 1% of the time, Pallas kernels for 9%

profile of v3, /device:TPU:1, one launch (start us, length us, event | category | flops | bytes accessed | tf_op | source)
XLA Modules:
  0.0 85.1 jit_solution(10338344011297302621)
XLA Ops:
  0.6 32.1 %all_gather.3.va.ta.tb.tc.td = bf16[128,2048]{1,0:T(8,128)(2,1)S(1)} all-gather(bf16[8,2048]{1,0:T(8,128)(2,1)} %bitcast.19), channel_id=1, replica_groups={{0,1,2,3,4,5,6,7,8,9,10,11,12,13,14,15},{16,17,18,19,20,21,22,23,24,25,..., dimensions={0}, use_global_device_ids=true | all-gather | bytes 557056 | tf_op jit(solution)/shard_map/all_gather | solution.py:105
  32.7 0.0 copy-start.1
  32.7 3.3 %collective-permute-start = (bf16[128,2048]{1,0:T(8,128)(2,1)S(1)}, bf16[128,2048]{1,0:T(8,128)(2,1)S(1)}, u32[]{:S(2)}, u32[]{:S(2)}) collective-permute-start(bf16[128,2048]{1,0:T(8,128)(2,1)S(1)} %all_gather.3.va.ta.tb.tc.td), channel_id=1, source_target_pairs={{0,16},{1,17},{2,18},{3,19},{4,20},{5,21},{6,22},{7,23},{8,24},{9,... | collective-permute-start | bytes 1572872 | tf_op jit(solution)/shard_map/ppermute | solution.py:107
  36.0 4.5 %collective-permute-start.1 = (bf16[128,2048]{1,0:T(8,128)(2,1)S(1)}, bf16[128,2048]{1,0:T(8,128)(2,1)S(1)}, u32[]{:S(2)}, u32[]{:S(2)}) collective-permute-start(bf16[128,2048]{1,0:T(8,128)(2,1)S(1)} %all_gather.3.va.ta.tb.tc.td), channel_id=1, source_target_pairs={{0,32},{1,33},{2,34},{3,35},{4,36},{5,37},{6,38},{7,39},{8,40},{9,... | collective-permute-start | bytes 1572872 | tf_op jit(solution)/shard_map/ppermute | solution.py:107
  40.6 3.0 %collective-permute-start.2 = (bf16[128,2048]{1,0:T(8,128)(2,1)S(1)}, bf16[128,2048]{1,0:T(8,128)(2,1)}, u32[]{:S(2)}, u32[]{:S(2)}) collective-permute-start(bf16[128,2048]{1,0:T(8,128)(2,1)S(1)} %all_gather.3.va.ta.tb.tc.td), channel_id=1, source_target_pairs={{0,48},{1,49},{2,50},{3,51},{4,52},{5,53},{6,54},{7,55},{8,56},{9,... | collective-permute-start | bytes 1572872 | tf_op jit(solution)/shard_map/ppermute | solution.py:107
  43.6 0.1 stack.31.place
  43.7 0.0 copy-start
  43.7 0.7 copy-done
  44.4 0.0 copy-start.2
  44.4 1.8 %pick_tiles.1 = bf16[8,4,16,256]{3,2,1,0:T(8,128)(2,1)} custom-call(s32[8]{0:T(128)S(1)} %stack.31.place, s32[2,8]{1,0:T(2,128)S(1)} %bitcast.16, bf16[128,2048]{1,0:T(8,128)(2,1)S(1)} %all_gather.3.va.ta.tb.tc.td, bf16[128,2048]{1,0:T(8,128)(2,1)S(1)} %all_gather.3.va.ta.tb.tc.td, bf16[128,2048]{1,0:T(8,128)(2,1)S(1)} %all_gather.3.va.ta.tb.tc.td, ...), custom_call_target="tpu_custom_call" | custom-call | tf_op jit(solution)/shard_map/pick_tiles/pallas_call | solution.py:116
  46.2 13.7 %all-to-all-start = ((bf16[32,16,256]{2,1,0:T(8,128)(2,1)}), bf16[32,16,256]{2,1,0:T(8,128)(2,1)S(1)}, u32[]{:S(2)}, u32[]{:S(2)}) async-start(bf16[32,16,256]{2,1,0:T(8,128)(2,1)} %bitcast.10), calls=%async_computation | async-start | bytes 524288 | tf_op jit(solution)/shard_map/all_to_all | solution.py:129
  59.9 8.8 %all-to-all-done = bf16[32,16,256]{2,1,0:T(8,128)(2,1)S(1)} async-done(((bf16[32,16,256]{2,1,0:T(8,128)(2,1)}), bf16[32,16,256]{2,1,0:T(8,128)(2,1)S(1)}, u32[]{:S(2)}, u32[]{:S(2)}) %all-to-all-start) | async-done | bytes 262176 | tf_op jit(solution)/shard_map/all_to_all | solution.py:129
  68.7 0.7 broadcast_in_dim.11
  69.4 3.9 %all-to-all-start.1 = ((bf16[8,64,256]{2,1,0:T(8,128)(2,1)}), bf16[8,64,256]{2,1,0:T(8,128)(2,1)S(1)}, u32[]{:S(2)}, u32[]{:S(2)}) async-start(bf16[8,64,256]{2,1,0:T(8,128)(2,1)} %broadcast_in_dim.11), calls=%async_computation.1 | async-start | bytes 524288 | tf_op jit(solution)/shard_map/all_to_all | solution.py:131
  73.3 0.0 collective-permute-done.vb
  73.3 0.0 collective-permute-done.1.vc
  73.3 0.0 collective-permute-done.2.vd
  73.3 0.0 copy-done.1
  73.3 0.0 copy-done.2
  73.3 5.4 %own_factors.1 = (bf16[1024,512]{1,0:T(8,128)(2,1)}, bf16[1024,512]{1,0:T(8,128)(2,1)}, bf16[1024,512]{1,0:T(8,128)(2,1)}, bf16[8,16,256]{2,1,0:T(8,128)(2,1)}) custom-call(s32[8]{0:T(128)S(1)} %stack.31.place, s32[2,8]{1,0:T(2,128)S(1)} %bitcast.17, bf16[3,512,512]{2,1,0:T(8,128)(2,1)S(1)} %copy-done.2, bf16[128,2048]{1,0:T(8,128)(2,1)S(1)} %all_gather.3.va.ta.tb.tc.td, ...), custom_call_target="tpu_custom_call" | custom-call | flops 8000000000 | bytes 8388608 | tf_op jit(solution)/shard_map/own_factors/pallas_call | solution.py:140
  78.8 1.1 %all-to-all-done.1.cuts = bf16[8,64,256]{2,1,0:T(8,128)(2,1)S(1)} async-done(((bf16[8,64,256]{2,1,0:T(8,128)(2,1)}), bf16[8,64,256]{2,1,0:T(8,128)(2,1)S(1)}, u32[]{:S(2)}, u32[]{:S(2)}) %all-to-all-start.1) | async-done | bytes 262176 | tf_op jit(solution)/shard_map/all_to_all | solution.py:131
  79.8 5.2 %tile_cores.1 = f32[8,256,256]{2,1,0:T(8,128)} custom-call(s32[8]{0:T(128)S(1)} %stack.31.place, bf16[3,512,512]{2,1,0:T(8,128)(2,1)S(1)} %copy-done.2, bf16[8,64,256]{2,1,0:T(8,128)(2,1)S(1)} %all-to-all-done.1.cuts, bf16[1024,512]{1,0:T(8,128)(2,1)} %get-tuple-element.7.wt, bf16[1024,512]{1,0:T(8,128)(2,1)} %get-tuple-element.8.lt, ...), custom_call_target="tpu_custom_call" | custom-call | flops 2000000000 | bytes 7340032 | tf_op jit(solution)/shard_map/tile_cores/pallas_call | solution.py:151
  (1 shorter events, 0.0 us)
Async XLA Ops:
  32.7 40.6 %copy-start.1 = (s32[8,2]{0,1:T(2,128)S(1)}, s32[8,2]{0,1:T(2,128)}, u32[]{:S(2)}) copy-start(s32[8,2]{0,1:T(2,128)} %param.5) | copy-start | bytes 196
  32.7 40.6 %collective-permute-start = (bf16[128,2048]{1,0:T(8,128)(2,1)S(1)}, bf16[128,2048]{1,0:T(8,128)(2,1)S(1)}, u32[]{:S(2)}, u32[]{:S(2)}) collective-permute-start(bf16[128,2048]{1,0:T(8,128)(2,1)S(1)} %all_gather.3.va.ta.tb.tc.td), channel_id=1, source_target_pairs={{0,16},{1,17},{2,18},{3,19},{4,20},{5,21},{6,22},{7,23},{8,24},{9,... | collective-permute-start | bytes 1572872 | tf_op jit(solution)/shard_map/ppermute | solution.py:107
  36.0 37.3 %collective-permute-start.1 = (bf16[128,2048]{1,0:T(8,128)(2,1)S(1)}, bf16[128,2048]{1,0:T(8,128)(2,1)S(1)}, u32[]{:S(2)}, u32[]{:S(2)}) collective-permute-start(bf16[128,2048]{1,0:T(8,128)(2,1)S(1)} %all_gather.3.va.ta.tb.tc.td), channel_id=1, source_target_pairs={{0,32},{1,33},{2,34},{3,35},{4,36},{5,37},{6,38},{7,39},{8,40},{9,... | collective-permute-start | bytes 1572872 | tf_op jit(solution)/shard_map/ppermute | solution.py:107
  40.6 32.7 %collective-permute-start.2 = (bf16[128,2048]{1,0:T(8,128)(2,1)S(1)}, bf16[128,2048]{1,0:T(8,128)(2,1)}, u32[]{:S(2)}, u32[]{:S(2)}) collective-permute-start(bf16[128,2048]{1,0:T(8,128)(2,1)S(1)} %all_gather.3.va.ta.tb.tc.td), channel_id=1, source_target_pairs={{0,48},{1,49},{2,50},{3,51},{4,52},{5,53},{6,54},{7,55},{8,56},{9,... | collective-permute-start | bytes 1572872 | tf_op jit(solution)/shard_map/ppermute | solution.py:107
  43.7 0.7 copy-start
  44.4 29.0 %copy-start.2 = (bf16[3,512,512]{2,1,0:T(8,128)(2,1)S(1)}, bf16[3,512,512]{2,1,0:T(8,128)(2,1)}, u32[]{:S(2)}) copy-start(bf16[3,512,512]{2,1,0:T(8,128)(2,1)} %diag.3) | copy-start | bytes 4718596
  46.2 22.5 %all-to-all-start = ((bf16[32,16,256]{2,1,0:T(8,128)(2,1)}), bf16[32,16,256]{2,1,0:T(8,128)(2,1)S(1)}, u32[]{:S(2)}, u32[]{:S(2)}) async-start(bf16[32,16,256]{2,1,0:T(8,128)(2,1)} %bitcast.10), calls=%async_computation | async-start | bytes 524288 | tf_op jit(solution)/shard_map/all_to_all | solution.py:129
  69.4 10.4 %all-to-all-start.1 = ((bf16[8,64,256]{2,1,0:T(8,128)(2,1)}), bf16[8,64,256]{2,1,0:T(8,128)(2,1)S(1)}, u32[]{:S(2)}, u32[]{:S(2)}) async-start(bf16[8,64,256]{2,1,0:T(8,128)(2,1)} %broadcast_in_dim.11), calls=%async_computation.1 | async-start | bytes 524288 | tf_op jit(solution)/shard_map/all_to_all | solution.py:131

commit v4 on v3

--- a/solution.py
+++ b/solution.py
@@ -24,39 +24,39 @@
         picked[:, y] = kept.reshape(picked.shape[0], picked.shape[2], picked.shape[3])
 
 
+def spread_cut(place, cut, sent):
+    for p in range(sent.shape[0]):
+        sent[p] = cut[...]
+
+
 def own_factors(place, ranks, diag, va, vb, vc, vd, wt, lt, rt, share, block):
-    step = pl.program_id(0)
-    piece = share.shape[1]
-    nloc, rank = block.shape[0], block.shape[1] // 4
+    tiles, piece, wide = share.shape
+    nloc, rank = block.shape[0], wide // 2
     part = nloc // Y
-    q = place[0]
     half = nloc // piece
-    rows = pl.ds(pl.multiple_of(lax.rem(q, half) * piece, piece), piece)
-    first = q < half
-    row = lax.broadcasted_iota(jnp.int32, (2 * rank, 1), 0)
-    lane = lax.broadcasted_iota(jnp.int32, (1, 2 * rank), 1)
+    rows = pl.ds(pl.multiple_of(lax.rem(place[0], half) * piece, piece), piece)
+    first = place[0] < half
 
-    def keep(at, k):
-        one, two = ranks[k, 2 * step], ranks[k, 2 * step + 1]
-        return at < jnp.where(at < rank, one, two + rank)
+    def masked(k, axis, x):
+        at = lax.broadcasted_iota(jnp.int32, (rank, 1) if axis == 0 else (1, rank), axis)
+        cuts = [lax.slice_in_dim(x, t * rank, (t + 1) * rank, axis=axis) for t in range(tiles)]
+        return jnp.concatenate([jnp.where(at < ranks[k, t], cut, 0.0) for t, cut in enumerate(cuts)], axis)
 
     for d, v in enumerate((va, vb, vc, vd)):
         source = lax.rem(place[3] + Y - d, Y)
         block[pl.ds(pl.multiple_of(source * part, part), part), :] = v[...]
-    v0 = jnp.concatenate([block[:, :rank], block[:, 2 * rank : 3 * rank]], 1)
-    v1 = jnp.concatenate([block[:, rank : 2 * rank], block[:, 3 * rank :]], 1)
-    w = dot(v0, diag[0], 0, 1)
-    w = jnp.where(keep(row, 0), w, 0.0).astype(BF16)
+    v0 = jnp.concatenate([block[:, t * wide : t * wide + rank] for t in range(tiles)], 1)
+    v1 = jnp.concatenate([block[:, t * wide + rank : (t + 1) * wide] for t in range(tiles)], 1)
+    w = masked(0, 0, dot(v0, diag[0], 0, 1)).astype(BF16)
     wt[...] = w
     lt[...] = dot(w, diag[1], 1, 1).astype(BF16)
-    r = dot(v1, diag[2], 0, 1)
-    rt[...] = jnp.where(keep(row, 1), r, 0.0).astype(BF16)
-    top = jnp.where(keep(lane, 0), dot(diag[0, rows, :], v0, 1, 0), 0.0)
+    rt[...] = masked(1, 0, dot(v1, diag[2], 0, 1)).astype(BF16)
+    top = masked(0, 1, dot(diag[0, rows, :], v0, 1, 0))
     low = dot(diag[1, rows, :], w, 1, 1)
-    side = jnp.where(keep(lane, 1), dot(diag[2, rows, :], v1, 1, 0), 0.0)
+    side = masked(1, 1, dot(diag[2, rows, :], v1, 1, 0))
     left = jnp.where(first, top, low).astype(BF16)
     right = jnp.where(first, 0.0, side).astype(BF16)
-    for t in range(2):
+    for t in range(tiles):
         cut = slice(t * rank, (t + 1) * rank)
         share[t, :, :rank] = left[:, cut]
         share[t, :, rank:] = right[:, cut]
@@ -64,7 +64,7 @@
 
 def tile_cores(place, diag, cuts, wt, lt, rt, cores, column, wc, lrc):
     step = pl.program_id(0)
-    rank = wc.shape[1]
+    some, rank = cores.shape[0], wc.shape[1]
 
     @pl.when(step == 0)
     def _():
@@ -81,9 +81,9 @@
     both = dot(lt[...], lrc[...], 1, 0)
     corner = dot(wt[...], wc[...], 1, 0)
     below = dot(rt[...], lrc[...], 1, 0)
-    for t in range(2):
+    for t in range(some):
         cut = slice(t * rank, (t + 1) * rank)
-        active = (2 * step + t) * place[2] + place[1] > place[0]
+        active = (some * step + t) * place[2] + place[1] > place[0]
         cores[t, :rank, :rank] = jnp.where(active, both[cut, :rank] + corner[cut], 0.0)
         cores[t, :rank, rank:] = jnp.where(active, both[cut, rank:], 0.0)
         cores[t, rank:, :] = jnp.where(active, below[cut], 0.0)
@@ -100,7 +100,7 @@
     wide = pair * rank
     ycol, zcol = qcol // Z, qcol % Z
     local = [(y * Z + zcol) // nrow for y in range(Y)]
-    place = jnp.stack([qcol, prow, jnp.int32(nrow), ycol] + local).astype(jnp.int32)
+    place = jnp.stack([qcol, prow, jnp.int32(nrow), ycol] + local + [zcol % nrow]).astype(jnp.int32)
     flat = panel_v.transpose(2, 0, 1, 3).reshape(mine, tiles * wide)
     slab = lax.all_gather(flat, "col", axis=0, tiled=True, axis_index_groups=along_z)
     parts = [slab] + [
@@ -124,35 +124,48 @@
         out_shape=jax.ShapeDtypeStruct((nrow, Y, rows, wide), BF16),
         compiler_params=pltpu.CompilerParams(vmem_limit_bytes=4 << 20),
         name="pick_tiles",
-    )(place, ranks.T, *[slab] * Y)
+    )(place, pltpu.with_memory_space_constraint(ranks.T, pltpu.HBM), *[slab] * Y)
     picked = picked.reshape(nrow * Y, rows, wide)
     cut = lax.all_to_all(picked, ("row", "col"), 0, 0, axis_index_groups=across)
-    cut = lax.dynamic_slice_in_dim(cut, zcol % nrow * Y, Y, 0).reshape(1, Y * rows, wide)
-    cuts = lax.all_to_all(jnp.broadcast_to(cut, (nrow,) + cut.shape[1:]), "row", 0, 0)
+    sent = pl.pallas_call(
+        spread_cut,
+        grid_spec=pltpu.PrefetchScalarGridSpec(
+            num_scalar_prefetch=1,
+            grid=(1,),
+            in_specs=[pl.BlockSpec((Y, rows, wide), lambda i, where: (where[8], 0, 0))],
+            out_specs=pl.BlockSpec((nrow, Y, rows, wide), lambda i, where: (0, 0, 0, 0)),
+        ),
+        out_shape=jax.ShapeDtypeStruct((nrow, Y, rows, wide), BF16),
+        compiler_params=pltpu.CompilerParams(vmem_limit_bytes=4 << 20),
+        cost_estimate=pl.CostEstimate(flops=0, bytes_accessed=1 << 20, transcendentals=0),
+        name="spread_cut",
+    )(place, cut)
+    cuts = lax.all_to_all(sent.reshape(nrow, Y * rows, wide), "row", 0, 0)
 
-    steps = tiles // 2
+    some = tiles // 2
     scalars = pl.BlockSpec(memory_space=pltpu.SMEM)
     matrices = pl.BlockSpec(diag_factors.shape, lambda i: (0, 0, 0))
-    turned = pl.BlockSpec((wide, nloc), lambda i: (i, 0))
+    turned = pl.BlockSpec((some * rank, nloc), lambda i: (i, 0))
+    full = pl.BlockSpec((tiles * rank, nloc), lambda i: (0, 0))
     lying = pltpu.HBM((tiles * rank, nloc), BF16)
     piece = 2 * nloc // ncol
-    limits = pltpu.CompilerParams(vmem_limit_bytes=16 << 20)
+    limits = pltpu.CompilerParams(vmem_limit_bytes=24 << 20)
     wt, lt, rt, share = pl.pallas_call(
         own_factors,
-        grid=(steps,),
-        in_specs=[scalars, scalars, matrices] + [pl.BlockSpec((nloc // Y, 2 * wide), lambda i: (0, i))] * Y,
-        out_specs=[turned] * 3 + [pl.BlockSpec((2, piece, wide), lambda i: (i, 0, 0))],
+        grid=(1,),
+        in_specs=[scalars, scalars, matrices] + [pl.BlockSpec(slab.shape, lambda i: (0, 0))] * Y,
+        out_specs=[full] * 3 + [pl.BlockSpec((tiles, piece, wide), lambda i: (0, 0, 0))],
         out_shape=[lying] * 3 + [jax.ShapeDtypeStruct((tiles, piece, wide), BF16)],
-        scratch_shapes=[pltpu.VMEM((nloc, 2 * wide), BF16)],
+        scratch_shapes=[pltpu.VMEM((nloc, tiles * wide), BF16)],
         compiler_params=limits,
         cost_estimate=pl.CostEstimate(flops=8 * 10**9, bytes_accessed=8 << 20, transcendentals=0),
         name="own_factors",
     )(place, ranks.T, diag_factors, *parts)
     cores = pl.pallas_call(
         tile_cores,
-        grid=(steps,),
+        grid=(tiles // some,),
         in_specs=[scalars, matrices, pl.BlockSpec(cuts.shape, lambda i: (0, 0, 0))] + [turned] * 3,
-        out_specs=pl.BlockSpec((2, wide, wide), lambda i: (i, 0, 0)),
+        out_specs=pl.BlockSpec((some, wide, wide), lambda i: (i, 0, 0)),
         out_shape=jax.ShapeDtypeStruct((tiles, wide, wide), jnp.float32),
         scratch_shapes=[pltpu.VMEM((nloc, n), BF16) for n in (wide, rank, wide)],
         compiler_params=limits,

time: 85.6 us -> 83.9 us (0.980)
  blocking collectives: 32.1 us -> 54.3 us
  starting transfers between devices: 28.4 us -> 14.7 us
  waiting for transfers between devices: 9.87 us -> 2.07 us
  local copies, waits for them, and re-layouts: 1.5 us -> 0.09 us
  Pallas kernels: 12.5 us -> 11.1 us
    all_to_all x0 -> x1, blocking collectives: none -> 22.3 us  [shards(): cut = lax.all_to_all(picked, ('row', 'col'), 0, 0, axis_index_groups=across)]
    all_to_all x2 -> x1, starting transfers between devices: 17.5 us -> 3.91 us  [shards(): cuts = lax.all_to_all(sent.reshape(nrow, Y * rows, wide), 'row', 0, 0)]
    all_to_all x2 -> x1, waiting for transfers between devices: 9.86 us -> 2.07 us  [shards(): cuts = lax.all_to_all(sent.reshape(nrow, Y * rows, wide), 'row', 0, 0)]
    pallas_call x2 -> x3, Pallas kernels: 10.6 us -> 9.83 us  [the longest x1 4.4 us: shards(): pl.pallas_call(own_factors, grid=(1,), in_specs=[scalars, scalars, matric...]
  transfers between devices with their start and end apart: 5 -> 4, of which waited for: 2 -> 1; matrix products, arithmetic and copies ran while one was open for 1% -> 0% of each run, Pallas kernels for 9% -> 8%
where the time goes in v4:
time: 83.9 us; the launch traced here: 83.1 us
  blocking collectives  54.3 us (65%)
  starting transfers between devices  14.7 us (18%)
  Pallas kernels  11.1 us (13%)
  waiting for transfers between devices  2.07 us (2%)
    all_gather x1, blocking collectives, shards(): lax.all_gather(flat, 'col', axis=0, tiled=True, axis_index_groups=along_z)  32.1 us
    all_to_all x1, blocking collectives, shards(): cut = lax.all_to_all(picked, ('row', 'col'), 0, 0, axis_index_groups=across)  22.3 us
    ppermute x3, starting transfers between devices, shards(): lax.ppermute(slab, 'col', [(y * Z + z, (y + d) % Y * Z + z) for y in rang...  10.8 us
    pallas_call x1, Pallas kernels, shards(): pl.pallas_call(own_factors, grid=(1,), in_specs=[scalars, scalars, matric...  4.4 us
    pallas_call x1, Pallas kernels, shards(): pl.pallas_call(tile_cores, grid=(tiles // some,), in_specs=[scalars, matr...  4.17 us
    all_to_all x1, starting transfers between devices, shards(): cuts = lax.all_to_all(sent.reshape(nrow, Y * rows, wide), 'row', 0, 0)  3.91 us
    all_to_all x1, waiting for transfers between devices, shards(): cuts = lax.all_to_all(sent.reshape(nrow, Y * rows, wide), 'row', 0, 0)  2.07 us
  transfers between devices with their start and end apart: 4, of which 1 were waited for; matrix products, arithmetic and copies ran while one was open for 0% of the time, Pallas kernels for 8%

profile of v4, /device:TPU:1, one launch (start us, length us, event | category | flops | bytes accessed | tf_op | source)
XLA Modules:
  0.0 83.1 jit_solution(5104584776478072192)
XLA Ops:
  0.6 32.1 %all_gather.3.va.ta.tb.tc.td = bf16[128,2048]{1,0:T(8,128)(2,1)S(1)} all-gather(bf16[8,2048]{1,0:T(8,128)(2,1)} %bitcast.20), channel_id=1, replica_groups={{0,1,2,3,4,5,6,7,8,9,10,11,12,13,14,15},{16,17,18,19,20,21,22,23,24,25,..., dimensions={0}, use_global_device_ids=true | all-gather | bytes 557056 | tf_op jit(solution)/shard_map/all_gather | solution.py:105
  32.7 0.0 copy-start
  32.7 0.0 copy-start.1
  32.7 3.3 %collective-permute-start = (bf16[128,2048]{1,0:T(8,128)(2,1)S(1)}, bf16[128,2048]{1,0:T(8,128)(2,1)S(1)}, u32[]{:S(2)}, u32[]{:S(2)}) collective-permute-start(bf16[128,2048]{1,0:T(8,128)(2,1)S(1)} %all_gather.3.va.ta.tb.tc.td), channel_id=1, source_target_pairs={{0,16},{1,17},{2,18},{3,19},{4,20},{5,21},{6,22},{7,23},{8,24},{9,... | collective-permute-start | bytes 1572872 | tf_op jit(solution)/shard_map/ppermute | solution.py:107
  36.0 4.5 %collective-permute-start.1 = (bf16[128,2048]{1,0:T(8,128)(2,1)S(1)}, bf16[128,2048]{1,0:T(8,128)(2,1)S(1)}, u32[]{:S(2)}, u32[]{:S(2)}) collective-permute-start(bf16[128,2048]{1,0:T(8,128)(2,1)S(1)} %all_gather.3.va.ta.tb.tc.td), channel_id=1, source_target_pairs={{0,32},{1,33},{2,34},{3,35},{4,36},{5,37},{6,38},{7,39},{8,40},{9,... | collective-permute-start | bytes 1572872 | tf_op jit(solution)/shard_map/ppermute | solution.py:107
  40.6 3.0 %collective-permute-start.2 = (bf16[128,2048]{1,0:T(8,128)(2,1)S(1)}, bf16[128,2048]{1,0:T(8,128)(2,1)}, u32[]{:S(2)}, u32[]{:S(2)}) collective-permute-start(bf16[128,2048]{1,0:T(8,128)(2,1)S(1)} %all_gather.3.va.ta.tb.tc.td), channel_id=1, source_target_pairs={{0,48},{1,49},{2,50},{3,51},{4,52},{5,53},{6,54},{7,55},{8,56},{9,... | collective-permute-start | bytes 1572872 | tf_op jit(solution)/shard_map/ppermute | solution.py:107
  43.6 0.1 stack.35.place
  43.7 1.3 %pick_tiles.1 = bf16[8,4,16,256]{3,2,1,0:T(8,128)(2,1)S(1)} custom-call(s32[9]{0:T(128)S(1)} %stack.35.place, s32[2,8]{1,0:T(2,128)} %bitcast.18, bf16[128,2048]{1,0:T(8,128)(2,1)S(1)} %all_gather.3.va.ta.tb.tc.td, bf16[128,2048]{1,0:T(8,128)(2,1)S(1)} %all_gather.3.va.ta.tb.tc.td, bf16[128,2048]{1,0:T(8,128)(2,1)S(1)} %all_gather.3.va.ta.tb.tc.td, ...), custom_call_target="tpu_custom_call" | custom-call | tf_op jit(solution)/shard_map/pick_tiles/pallas_call | solution.py:116
  45.0 22.3 %all_to_all.10.cut = bf16[32,16,256]{2,1,0:T(8,128)(2,1)S(1)} all-to-all(bf16[32,16,256]{2,1,0:T(8,128)(2,1)S(1)} %bitcast.17), channel_id=1, replica_groups={{0,16,32,48,64,80,96,112,128,144,160,176,192,208,224,240,256,272,288,30..., dimensions={0} | all-to-all | bytes 524288 | tf_op jit(solution)/shard_map/all_to_all | solution.py:129
  67.2 1.3 %spread_cut.1 = bf16[8,4,16,256]{3,2,1,0:T(8,128)(2,1)} custom-call(s32[9]{0:T(128)S(1)} %stack.35.place, bf16[32,16,256]{2,1,0:T(8,128)(2,1)S(1)} %all_to_all.10.cut), custom_call_target="tpu_custom_call" | custom-call | bytes 1048576 | tf_op jit(solution)/shard_map/spread_cut/pallas_call | solution.py:130
  68.5 3.9 %all-to-all-start.1 = ((bf16[8,64,256]{2,1,0:T(8,128)(2,1)}), bf16[8,64,256]{2,1,0:T(8,128)(2,1)S(1)}, u32[]{:S(2)}, u32[]{:S(2)}) async-start(bf16[8,64,256]{2,1,0:T(8,128)(2,1)} %bitcast.12), calls=%async_computation.1 | async-start | bytes 524288 | tf_op jit(solution)/shard_map/all_to_all | solution.py:143
  72.4 0.0 collective-permute-done.vb
  72.4 0.0 collective-permute-done.1.vc
  72.4 0.0 collective-permute-done.2.vd
  72.4 0.0 copy-done
  72.4 0.0 copy-done.1
  72.5 4.4 %own_factors.1 = (bf16[1024,512]{1,0:T(8,128)(2,1)}, bf16[1024,512]{1,0:T(8,128)(2,1)}, bf16[1024,512]{1,0:T(8,128)(2,1)}, bf16[8,16,256]{2,1,0:T(8,128)(2,1)}) custom-call(s32[9]{0:T(128)S(1)} %stack.35.place, s32[2,8]{1,0:T(2,128)S(1)} %bitcast.19, bf16[3,512,512]{2,1,0:T(8,128)(2,1)S(1)} %copy-done.1, bf16[128,2048]{1,0:T(8,128)(2,1)S(1)} %all_gather.3.va.ta.tb.tc.td, ...), custom_call_target="tpu_custom_call" | custom-call | flops 8000000000 | bytes 8388608 | tf_op jit(solution)/shard_map/own_factors/pallas_call | solution.py:153
  76.8 2.1 %all-to-all-done.1.cuts = bf16[8,64,256]{2,1,0:T(8,128)(2,1)S(1)} async-done(((bf16[8,64,256]{2,1,0:T(8,128)(2,1)}), bf16[8,64,256]{2,1,0:T(8,128)(2,1)S(1)}, u32[]{:S(2)}, u32[]{:S(2)}) %all-to-all-start.1) | async-done | bytes 262176 | tf_op jit(solution)/shard_map/all_to_all | solution.py:143
  78.9 4.2 %tile_cores.1 = f32[8,256,256]{2,1,0:T(8,128)} custom-call(s32[9]{0:T(128)S(1)} %stack.35.place, bf16[3,512,512]{2,1,0:T(8,128)(2,1)S(1)} %copy-done.1, bf16[8,64,256]{2,1,0:T(8,128)(2,1)S(1)} %all-to-all-done.1.cuts, bf16[1024,512]{1,0:T(8,128)(2,1)} %get-tuple-element.7.wt, bf16[1024,512]{1,0:T(8,128)(2,1)} %get-tuple-element.8.lt, ...), custom_call_target="tpu_custom_call" | custom-call | flops 2000000000 | bytes 7340032 | tf_op jit(solution)/shard_map/tile_cores/pallas_call | solution.py:164
Async XLA Ops:
  32.7 39.7 %copy-start = (s32[8,2]{0,1:T(2,128)S(1)}, s32[8,2]{0,1:T(2,128)}, u32[]{:S(2)}) copy-start(s32[8,2]{0,1:T(2,128)} %param.5) | copy-start | bytes 196
  32.7 39.7 %copy-start.1 = (bf16[3,512,512]{2,1,0:T(8,128)(2,1)S(1)}, bf16[3,512,512]{2,1,0:T(8,128)(2,1)}, u32[]{:S(2)}) copy-start(bf16[3,512,512]{2,1,0:T(8,128)(2,1)} %diag.3) | copy-start | bytes 4718596
  32.7 39.7 %collective-permute-start = (bf16[128,2048]{1,0:T(8,128)(2,1)S(1)}, bf16[128,2048]{1,0:T(8,128)(2,1)S(1)}, u32[]{:S(2)}, u32[]{:S(2)}) collective-permute-start(bf16[128,2048]{1,0:T(8,128)(2,1)S(1)} %all_gather.3.va.ta.tb.tc.td), channel_id=1, source_target_pairs={{0,16},{1,17},{2,18},{3,19},{4,20},{5,21},{6,22},{7,23},{8,24},{9,... | collective-permute-start | bytes 1572872 | tf_op jit(solution)/shard_map/ppermute | solution.py:107
  36.0 36.4 %collective-permute-start.1 = (bf16[128,2048]{1,0:T(8,128)(2,1)S(1)}, bf16[128,2048]{1,0:T(8,128)(2,1)S(1)}, u32[]{:S(2)}, u32[]{:S(2)}) collective-permute-start(bf16[128,2048]{1,0:T(8,128)(2,1)S(1)} %all_gather.3.va.ta.tb.tc.td), channel_id=1, source_target_pairs={{0,32},{1,33},{2,34},{3,35},{4,36},{5,37},{6,38},{7,39},{8,40},{9,... | collective-permute-start | bytes 1572872 | tf_op jit(solution)/shard_map/ppermute | solution.py:107
  40.6 31.9 %collective-permute-start.2 = (bf16[128,2048]{1,0:T(8,128)(2,1)S(1)}, bf16[128,2048]{1,0:T(8,128)(2,1)}, u32[]{:S(2)}, u32[]{:S(2)}) collective-permute-start(bf16[128,2048]{1,0:T(8,128)(2,1)S(1)} %all_gather.3.va.ta.tb.tc.td), channel_id=1, source_target_pairs={{0,48},{1,49},{2,50},{3,51},{4,52},{5,53},{6,54},{7,55},{8,56},{9,... | collective-permute-start | bytes 1572872 | tf_op jit(solution)/shard_map/ppermute | solution.py:107
  68.5 10.4 %all-to-all-start.1 = ((bf16[8,64,256]{2,1,0:T(8,128)(2,1)}), bf16[8,64,256]{2,1,0:T(8,128)(2,1)S(1)}, u32[]{:S(2)}, u32[]{:S(2)}) async-start(bf16[8,64,256]{2,1,0:T(8,128)(2,1)} %bitcast.12), calls=%async_computation.1 | async-start | bytes 524288 | tf_op jit(solution)/shard_map/all_to_all | solution.py:143

commit v5 on v4

--- a/solution.py
+++ b/solution.py
@@ -127,6 +127,7 @@
     )(place, pltpu.with_memory_space_constraint(ranks.T, pltpu.HBM), *[slab] * Y)
     picked = picked.reshape(nrow * Y, rows, wide)
     cut = lax.all_to_all(picked, ("row", "col"), 0, 0, axis_index_groups=across)
+    cut, parts[2], parts[1] = lax.optimization_barrier((cut, parts[2], parts[1]))
     sent = pl.pallas_call(
         spread_cut,
         grid_spec=pltpu.PrefetchScalarGridSpec(
@@ -137,7 +138,7 @@
         ),
         out_shape=jax.ShapeDtypeStruct((nrow, Y, rows, wide), BF16),
         compiler_params=pltpu.CompilerParams(vmem_limit_bytes=4 << 20),
-        cost_estimate=pl.CostEstimate(flops=0, bytes_accessed=1 << 20, transcendentals=0),
+        cost_estimate=pl.CostEstimate(flops=20 * 10**9, bytes_accessed=1 << 20, transcendentals=0),
         name="spread_cut",
     )(place, cut)
     cuts = lax.all_to_all(sent.reshape(nrow, Y * rows, wide), "row", 0, 0)

time: 83.9 us -> 83.4 us (level)
  blocking collectives: 54.3 us -> 32.1 us
  starting transfers between devices: 14.7 us -> 30.6 us
  waiting for transfers between devices: 2.07 us -> 7.65 us
    all_to_all x1 -> x0, blocking collectives: 22.3 us -> none  [shards(): cut = lax.all_to_all(picked, ('row', 'col'), 0, 0, axis_index_groups=across)]
    all_to_all x0 -> x1, starting transfers between devices: none -> 14 us  [shards(): cut = lax.all_to_all(picked, ('row', 'col'), 0, 0, axis_index_groups=across)]
    all_to_all x0 -> x1, waiting for transfers between devices: none -> 4.14 us  [shards(): cut = lax.all_to_all(picked, ('row', 'col'), 0, 0, axis_index_groups=across)]
    ppermute x3, waiting for transfers between devices: 0.01 us -> 3.51 us  [shards(): lax.ppermute(slab, 'col', [(y * Z + z, (y + d) % Y * Z + z) for y in rang...]
    all_to_all x1, waiting for transfers between devices: 2.07 us -> 0.01 us  [shards(): cuts = lax.all_to_all(sent.reshape(nrow, Y * rows, wide), 'row', 0, 0)]
    ppermute x3, starting transfers between devices: 10.8 us -> 12.4 us  [shards(): lax.ppermute(slab, 'col', [(y * Z + z, (y + d) % Y * Z + z) for y in rang...]
  transfers between devices with their start and end apart: 4 -> 5, of which waited for: 1 -> 2; matrix products, arithmetic and copies ran while one was open for 0% -> 0% of each run, Pallas kernels for 8% -> 9%
where the time goes in v5:
time: 83.4 us; the launch traced here: 82.9 us
  blocking collectives  32.1 us (38%)
  starting transfers between devices  30.6 us (37%)
  Pallas kernels  11.8 us (14%)
  waiting for transfers between devices  7.65 us (9%)
    all_gather x1, blocking collectives, shards(): lax.all_gather(flat, 'col', axis=0, tiled=True, axis_index_groups=along_z)  32.1 us
    all_to_all x1, starting transfers between devices, shards(): cut = lax.all_to_all(picked, ('row', 'col'), 0, 0, axis_index_groups=across)  14 us
    ppermute x3, starting transfers between devices, shards(): lax.ppermute(slab, 'col', [(y * Z + z, (y + d) % Y * Z + z) for y in rang...  12.4 us
    pallas_call x1, Pallas kernels, shards(): pl.pallas_call(own_factors, grid=(1,), in_specs=[scalars, scalars, matric...  4.4 us
    pallas_call x1, Pallas kernels, shards(): pl.pallas_call(tile_cores, grid=(tiles // some,), in_specs=[scalars, matr...  4.17 us
    all_to_all x1, starting transfers between devices, shards(): cuts = lax.all_to_all(sent.reshape(nrow, Y * rows, wide), 'row', 0, 0)  4.16 us
    all_to_all x1, waiting for transfers between devices, shards(): cut = lax.all_to_all(picked, ('row', 'col'), 0, 0, axis_index_groups=across)  4.14 us
    ppermute x3, waiting for transfers between devices, shards(): lax.ppermute(slab, 'col', [(y * Z + z, (y + d) % Y * Z + z) for y in rang...  3.51 us
  transfers between devices with their start and end apart: 5, of which 2 were waited for; matrix products, arithmetic and copies ran while one was open for 0% of the time, Pallas kernels for 9%

profile of v5, /device:TPU:1, one launch (start us, length us, event | category | flops | bytes accessed | tf_op | source)
XLA Modules:
  0.0 82.9 jit_solution(17285634432736741595)
XLA Ops:
  0.6 32.1 %all_gather.3.ta.tb.tc.td.va = bf16[128,2048]{1,0:T(8,128)(2,1)S(1)} all-gather(bf16[8,2048]{1,0:T(8,128)(2,1)} %bitcast.19), channel_id=1, replica_groups={{0,1,2,3,4,5,6,7,8,9,10,11,12,13,14,15},{16,17,18,19,20,21,22,23,24,25,..., dimensions={0}, use_global_device_ids=true | all-gather | bytes 557056 | tf_op jit(solution)/shard_map/all_gather | solution.py:105
  32.7 3.2 %collective-permute-start.1 = (bf16[128,2048]{1,0:T(8,128)(2,1)S(1)}, bf16[128,2048]{1,0:T(8,128)(2,1)S(1)}, u32[]{:S(2)}, u32[]{:S(2)}) collective-permute-start(bf16[128,2048]{1,0:T(8,128)(2,1)S(1)} %all_gather.3.ta.tb.tc.td.va), channel_id=1, source_target_pairs={{0,16},{1,17},{2,18},{3,19},{4,20},{5,21},{6,22},{7,23},{8,24},{9,... | collective-permute-start | bytes 1572872 | tf_op jit(solution)/shard_map/ppermute | solution.py:107
  35.9 4.5 %collective-permute-start = (bf16[128,2048]{1,0:T(8,128)(2,1)S(1)}, bf16[128,2048]{1,0:T(8,128)(2,1)S(1)}, u32[]{:S(2)}, u32[]{:S(2)}) collective-permute-start(bf16[128,2048]{1,0:T(8,128)(2,1)S(1)} %all_gather.3.ta.tb.tc.td.va), channel_id=1, source_target_pairs={{0,32},{1,33},{2,34},{3,35},{4,36},{5,37},{6,38},{7,39},{8,40},{9,... | collective-permute-start | bytes 1572872 | tf_op jit(solution)/shard_map/ppermute | solution.py:107
  40.5 0.1 stack.35.place
  40.6 2.0 %pick_tiles.1 = bf16[8,4,16,256]{3,2,1,0:T(8,128)(2,1)} custom-call(s32[9]{0:T(128)S(1)} %stack.35.place, s32[2,8]{1,0:T(2,128)} %bitcast.17, bf16[128,2048]{1,0:T(8,128)(2,1)S(1)} %all_gather.3.ta.tb.tc.td.va, bf16[128,2048]{1,0:T(8,128)(2,1)S(1)} %all_gather.3.ta.tb.tc.td.va, bf16[128,2048]{1,0:T(8,128)(2,1)S(1)} %all_gather.3.ta.tb.tc.td.va, ...), custom_call_target="tpu_custom_call" | custom-call | tf_op jit(solution)/shard_map/pick_tiles/pallas_call | solution.py:116
  42.5 14.0 %all-to-all-start = ((bf16[32,16,256]{2,1,0:T(8,128)(2,1)}), bf16[32,16,256]{2,1,0:T(8,128)(2,1)S(1)}, u32[]{:S(2)}, u32[]{:S(2)}) async-start(bf16[32,16,256]{2,1,0:T(8,128)(2,1)} %bitcast.11), calls=%async_computation | async-start | bytes 524288 | tf_op jit(solution)/shard_map/all_to_all | solution.py:129
  56.6 0.0 copy-start
  56.6 0.0 copy-start.1
  56.6 4.6 %collective-permute-start.2 = (bf16[128,2048]{1,0:T(8,128)(2,1)S(1)}, bf16[128,2048]{1,0:T(8,128)(2,1)}, u32[]{:S(2)}, u32[]{:S(2)}) collective-permute-start(bf16[128,2048]{1,0:T(8,128)(2,1)S(1)} %all_gather.3.ta.tb.tc.td.va), channel_id=1, source_target_pairs={{0,48},{1,49},{2,50},{3,51},{4,52},{5,53},{6,54},{7,55},{8,56},{9,... | collective-permute-start | bytes 1572872 | tf_op jit(solution)/shard_map/ppermute | solution.py:107
  61.3 4.1 %all-to-all-done.cut = bf16[32,16,256]{2,1,0:T(8,128)(2,1)S(1)} async-done(((bf16[32,16,256]{2,1,0:T(8,128)(2,1)}), bf16[32,16,256]{2,1,0:T(8,128)(2,1)S(1)}, u32[]{:S(2)}, u32[]{:S(2)}) %all-to-all-start) | async-done | bytes 262176 | tf_op jit(solution)/shard_map/all_to_all | solution.py:129
  65.4 0.0 collective-permute-done.1.vb
  65.4 0.0 collective-permute-done.vc
  65.4 1.3 %spread_cut.1 = bf16[8,4,16,256]{3,2,1,0:T(8,128)(2,1)} custom-call(s32[9]{0:T(128)S(1)} %stack.35.place, bf16[32,16,256]{2,1,0:T(8,128)(2,1)S(1)} %all-to-all-done.cut), custom_call_target="tpu_custom_call" | custom-call | flops 20000000000 | bytes 1048576 | tf_op jit(solution)/shard_map/spread_cut/pallas_call | solution.py:131
  66.7 4.2 %all-to-all-start.1 = ((bf16[8,64,256]{2,1,0:T(8,128)(2,1)}), bf16[8,64,256]{2,1,0:T(8,128)(2,1)S(1)}, u32[]{:S(2)}, u32[]{:S(2)}) async-start(bf16[8,64,256]{2,1,0:T(8,128)(2,1)} %bitcast.12), calls=%async_computation.1 | async-start | bytes 524288 | tf_op jit(solution)/shard_map/all_to_all | solution.py:144
  70.8 3.5 %collective-permute-done.2.vd = bf16[128,2048]{1,0:T(8,128)(2,1)} collective-permute-done((bf16[128,2048]{1,0:T(8,128)(2,1)S(1)}, bf16[128,2048]{1,0:T(8,128)(2,1)}, u32[]{:S(2)}, u32[]{:S(2)}) %collective-permute-start.2) | collective-permute-done | bytes 524320 | tf_op jit(solution)/shard_map/ppermute | solution.py:107
  74.3 0.0 copy-done
  74.4 0.0 copy-done.1
  74.4 4.4 %own_factors.1 = (bf16[1024,512]{1,0:T(8,128)(2,1)}, bf16[1024,512]{1,0:T(8,128)(2,1)}, bf16[1024,512]{1,0:T(8,128)(2,1)}, bf16[8,16,256]{2,1,0:T(8,128)(2,1)}) custom-call(s32[9]{0:T(128)S(1)} %stack.35.place, s32[2,8]{1,0:T(2,128)S(1)} %bitcast.18, bf16[3,512,512]{2,1,0:T(8,128)(2,1)S(1)} %copy-done.1, bf16[128,2048]{1,0:T(8,128)(2,1)S(1)} %all_gather.3.ta.tb.tc.td.va, ...), custom_call_target="tpu_custom_call" | custom-call | flops 8000000000 | bytes 8388608 | tf_op jit(solution)/shard_map/own_factors/pallas_call | solution.py:154
  78.7 0.0 all-to-all-done.1.cuts
  78.8 4.2 %tile_cores.1 = f32[8,256,256]{2,1,0:T(8,128)} custom-call(s32[9]{0:T(128)S(1)} %stack.35.place, bf16[3,512,512]{2,1,0:T(8,128)(2,1)S(1)} %copy-done.1, bf16[8,64,256]{2,1,0:T(8,128)(2,1)S(1)} %all-to-all-done.1.cuts, bf16[1024,512]{1,0:T(8,128)(2,1)} %get-tuple-element.13.wt, bf16[1024,512]{1,0:T(8,128)(2,1)} %get-tuple-element.14.lt, ...), custom_call_target="tpu_custom_call" | custom-call | flops 2000000000 | bytes 7340032 | tf_op jit(solution)/shard_map/tile_cores/pallas_call | solution.py:165
Async XLA Ops:
  32.7 32.7 %collective-permute-start.1 = (bf16[128,2048]{1,0:T(8,128)(2,1)S(1)}, bf16[128,2048]{1,0:T(8,128)(2,1)S(1)}, u32[]{:S(2)}, u32[]{:S(2)}) collective-permute-start(bf16[128,2048]{1,0:T(8,128)(2,1)S(1)} %all_gather.3.ta.tb.tc.td.va), channel_id=1, source_target_pairs={{0,16},{1,17},{2,18},{3,19},{4,20},{5,21},{6,22},{7,23},{8,24},{9,... | collective-permute-start | bytes 1572872 | tf_op jit(solution)/shard_map/ppermute | solution.py:107
  35.9 29.5 %collective-permute-start = (bf16[128,2048]{1,0:T(8,128)(2,1)S(1)}, bf16[128,2048]{1,0:T(8,128)(2,1)S(1)}, u32[]{:S(2)}, u32[]{:S(2)}) collective-permute-start(bf16[128,2048]{1,0:T(8,128)(2,1)S(1)} %all_gather.3.ta.tb.tc.td.va), channel_id=1, source_target_pairs={{0,32},{1,33},{2,34},{3,35},{4,36},{5,37},{6,38},{7,39},{8,40},{9,... | collective-permute-start | bytes 1572872 | tf_op jit(solution)/shard_map/ppermute | solution.py:107
  42.5 22.9 %all-to-all-start = ((bf16[32,16,256]{2,1,0:T(8,128)(2,1)}), bf16[32,16,256]{2,1,0:T(8,128)(2,1)S(1)}, u32[]{:S(2)}, u32[]{:S(2)}) async-start(bf16[32,16,256]{2,1,0:T(8,128)(2,1)} %bitcast.11), calls=%async_computation | async-start | bytes 524288 | tf_op jit(solution)/shard_map/all_to_all | solution.py:129
  56.6 17.7 %copy-start = (s32[8,2]{0,1:T(2,128)S(1)}, s32[8,2]{0,1:T(2,128)}, u32[]{:S(2)}) copy-start(s32[8,2]{0,1:T(2,128)} %param.5) | copy-start | bytes 196
  56.6 17.7 %copy-start.1 = (bf16[3,512,512]{2,1,0:T(8,128)(2,1)S(1)}, bf16[3,512,512]{2,1,0:T(8,128)(2,1)}, u32[]{:S(2)}) copy-start(bf16[3,512,512]{2,1,0:T(8,128)(2,1)} %diag.3) | copy-start | bytes 4718596
  56.6 17.7 %collective-permute-start.2 = (bf16[128,2048]{1,0:T(8,128)(2,1)S(1)}, bf16[128,2048]{1,0:T(8,128)(2,1)}, u32[]{:S(2)}, u32[]{:S(2)}) collective-permute-start(bf16[128,2048]{1,0:T(8,128)(2,1)S(1)} %all_gather.3.ta.tb.tc.td.va), channel_id=1, source_target_pairs={{0,48},{1,49},{2,50},{3,51},{4,52},{5,53},{6,54},{7,55},{8,56},{9,... | collective-permute-start | bytes 1572872 | tf_op jit(solution)/shard_map/ppermute | solution.py:107
  66.7 12.1 %all-to-all-start.1 = ((bf16[8,64,256]{2,1,0:T(8,128)(2,1)}), bf16[8,64,256]{2,1,0:T(8,128)(2,1)S(1)}, u32[]{:S(2)}, u32[]{:S(2)}) async-start(bf16[8,64,256]{2,1,0:T(8,128)(2,1)} %bitcast.12), calls=%async_computation.1 | async-start | bytes 524288 | tf_op jit(solution)/shard_map/all_to_all | solution.py:144

commit v6 on v5

--- a/solution.py
+++ b/solution.py
@@ -12,6 +12,16 @@
 
 def dot(a, b, ca, cb):
     return lax.dot_general(a, b, (((ca,), (cb,)), ((), ())), preferred_element_type=jnp.float32)
+
+
+def lower(v, a):
+    half = a.shape[0] // 2
+    return jnp.concatenate([dot(v[:half], a[:half, :half], 0, 1), dot(v, a[half:], 0, 1)], 1)
+
+
+def lower_times(a, v):
+    half = a.shape[0] // 2
+    return jnp.concatenate([dot(a[:half, :half], v[:half], 1, 0), dot(a[half:], v, 1, 0)], 0)
 
 
 def pick_tiles(place, ranks, ta, tb, tc, td, picked):
@@ -47,10 +57,10 @@
         block[pl.ds(pl.multiple_of(source * part, part), part), :] = v[...]
     v0 = jnp.concatenate([block[:, t * wide : t * wide + rank] for t in range(tiles)], 1)
     v1 = jnp.concatenate([block[:, t * wide + rank : (t + 1) * wide] for t in range(tiles)], 1)
-    w = masked(0, 0, dot(v0, diag[0], 0, 1)).astype(BF16)
+    w = masked(0, 0, lower(v0, diag[0])).astype(BF16)
     wt[...] = w
     lt[...] = dot(w, diag[1], 1, 1).astype(BF16)
-    rt[...] = masked(1, 0, dot(v1, diag[2], 0, 1)).astype(BF16)
+    rt[...] = masked(1, 0, lower(v1, diag[2])).astype(BF16)
     top = masked(0, 1, dot(diag[0, rows, :], v0, 1, 0))
     low = dot(diag[1, rows, :], w, 1, 1)
     side = masked(1, 1, dot(diag[2, rows, :], v1, 1, 0))
@@ -73,10 +83,10 @@
             for p in range(cuts.shape[0]):
                 at = (y * cuts.shape[0] + p) * rows
                 column[at : at + rows, :] = cuts[p, y * rows : (y + 1) * rows, :]
-        w = dot(diag[0], column[:, :rank], 1, 0).astype(BF16)
+        w = lower_times(diag[0], column[:, :rank]).astype(BF16)
         wc[...] = w
         lrc[:, :rank] = dot(diag[1], w, 1, 0).astype(BF16)
-        lrc[:, rank:] = dot(diag[2], column[:, rank:], 1, 0).astype(BF16)
+        lrc[:, rank:] = lower_times(diag[2], column[:, rank:]).astype(BF16)
 
     both = dot(lt[...], lrc[...], 1, 0)
     corner = dot(wt[...], wc[...], 1, 0)

time: 83.4 us -> 83.2 us (level)
  no operation moved by 1% of the time
where the time goes in v6:
time: 83.2 us; the launch traced here: 82.8 us
  blocking collectives  32.1 us (39%)
  starting transfers between devices  30.6 us (37%)
  Pallas kernels  11.7 us (14%)
  waiting for transfers between devices  7.65 us (9%)
    all_gather x1, blocking collectives, shards(): lax.all_gather(flat, 'col', axis=0, tiled=True, axis_index_groups=along_z)  32.1 us
    all_to_all x1, starting transfers between devices, shards(): cut = lax.all_to_all(picked, ('row', 'col'), 0, 0, axis_index_groups=across)  14 us
    ppermute x3, starting transfers between devices, shards(): lax.ppermute(slab, 'col', [(y * Z + z, (y + d) % Y * Z + z) for y in rang...  12.4 us
    pallas_call x1, Pallas kernels, shards(): pl.pallas_call(own_factors, grid=(1,), in_specs=[scalars, scalars, matric...  4.26 us
    all_to_all x1, starting transfers between devices, shards(): cuts = lax.all_to_all(sent.reshape(nrow, Y * rows, wide), 'row', 0, 0)  4.16 us
    pallas_call x1, Pallas kernels, shards(): pl.pallas_call(tile_cores, grid=(tiles // some,), in_specs=[scalars, matr...  4.16 us
    all_to_all x1, waiting for transfers between devices, shards(): cut = lax.all_to_all(picked, ('row', 'col'), 0, 0, axis_index_groups=across)  4.14 us
    ppermute x3, waiting for transfers between devices, shards(): lax.ppermute(slab, 'col', [(y * Z + z, (y + d) % Y * Z + z) for y in rang...  3.51 us
  transfers between devices with their start and end apart: 5, of which 2 were waited for; matrix products, arithmetic and copies ran while one was open for 0% of the time, Pallas kernels for 9%

profile of v6, /device:TPU:1, one launch (start us, length us, event | category | flops | bytes accessed | tf_op | source)
XLA Modules:
  0.0 82.8 jit_solution(4420892800257073438)
XLA Ops:
  0.6 32.1 %all_gather.3.ta.tb.tc.td.va = bf16[128,2048]{1,0:T(8,128)(2,1)S(1)} all-gather(bf16[8,2048]{1,0:T(8,128)(2,1)} %bitcast.19), channel_id=1, replica_groups={{0,1,2,3,4,5,6,7,8,9,10,11,12,13,14,15},{16,17,18,19,20,21,22,23,24,25,..., dimensions={0}, use_global_device_ids=true | all-gather | bytes 557056 | tf_op jit(solution)/shard_map/all_gather | solution.py:115
  32.7 3.2 %collective-permute-start.1 = (bf16[128,2048]{1,0:T(8,128)(2,1)S(1)}, bf16[128,2048]{1,0:T(8,128)(2,1)S(1)}, u32[]{:S(2)}, u32[]{:S(2)}) collective-permute-start(bf16[128,2048]{1,0:T(8,128)(2,1)S(1)} %all_gather.3.ta.tb.tc.td.va), channel_id=1, source_target_pairs={{0,16},{1,17},{2,18},{3,19},{4,20},{5,21},{6,22},{7,23},{8,24},{9,... | collective-permute-start | bytes 1572872 | tf_op jit(solution)/shard_map/ppermute | solution.py:117
  35.9 4.5 %collective-permute-start = (bf16[128,2048]{1,0:T(8,128)(2,1)S(1)}, bf16[128,2048]{1,0:T(8,128)(2,1)S(1)}, u32[]{:S(2)}, u32[]{:S(2)}) collective-permute-start(bf16[128,2048]{1,0:T(8,128)(2,1)S(1)} %all_gather.3.ta.tb.tc.td.va), channel_id=1, source_target_pairs={{0,32},{1,33},{2,34},{3,35},{4,36},{5,37},{6,38},{7,39},{8,40},{9,... | collective-permute-start | bytes 1572872 | tf_op jit(solution)/shard_map/ppermute | solution.py:117
  40.5 0.1 stack.35.place
  40.6 2.0 %pick_tiles.1 = bf16[8,4,16,256]{3,2,1,0:T(8,128)(2,1)} custom-call(s32[9]{0:T(128)S(1)} %stack.35.place, s32[2,8]{1,0:T(2,128)} %bitcast.17, bf16[128,2048]{1,0:T(8,128)(2,1)S(1)} %all_gather.3.ta.tb.tc.td.va, bf16[128,2048]{1,0:T(8,128)(2,1)S(1)} %all_gather.3.ta.tb.tc.td.va, bf16[128,2048]{1,0:T(8,128)(2,1)S(1)} %all_gather.3.ta.tb.tc.td.va, ...), custom_call_target="tpu_custom_call" | custom-call | tf_op jit(solution)/shard_map/pick_tiles/pallas_call | solution.py:126
  42.5 14.0 %all-to-all-start = ((bf16[32,16,256]{2,1,0:T(8,128)(2,1)}), bf16[32,16,256]{2,1,0:T(8,128)(2,1)S(1)}, u32[]{:S(2)}, u32[]{:S(2)}) async-start(bf16[32,16,256]{2,1,0:T(8,128)(2,1)} %bitcast.11), calls=%async_computation | async-start | bytes 524288 | tf_op jit(solution)/shard_map/all_to_all | solution.py:139
  56.6 0.0 copy-start
  56.6 0.0 copy-start.1
  56.6 4.6 %collective-permute-start.2 = (bf16[128,2048]{1,0:T(8,128)(2,1)S(1)}, bf16[128,2048]{1,0:T(8,128)(2,1)}, u32[]{:S(2)}, u32[]{:S(2)}) collective-permute-start(bf16[128,2048]{1,0:T(8,128)(2,1)S(1)} %all_gather.3.ta.tb.tc.td.va), channel_id=1, source_target_pairs={{0,48},{1,49},{2,50},{3,51},{4,52},{5,53},{6,54},{7,55},{8,56},{9,... | collective-permute-start | bytes 1572872 | tf_op jit(solution)/shard_map/ppermute | solution.py:117
  61.3 4.1 %all-to-all-done.cut = bf16[32,16,256]{2,1,0:T(8,128)(2,1)S(1)} async-done(((bf16[32,16,256]{2,1,0:T(8,128)(2,1)}), bf16[32,16,256]{2,1,0:T(8,128)(2,1)S(1)}, u32[]{:S(2)}, u32[]{:S(2)}) %all-to-all-start) | async-done | bytes 262176 | tf_op jit(solution)/shard_map/all_to_all | solution.py:139
  65.4 0.0 collective-permute-done.1.vb
  65.4 0.0 collective-permute-done.vc
  65.4 1.3 %spread_cut.1 = bf16[8,4,16,256]{3,2,1,0:T(8,128)(2,1)} custom-call(s32[9]{0:T(128)S(1)} %stack.35.place, bf16[32,16,256]{2,1,0:T(8,128)(2,1)S(1)} %all-to-all-done.cut), custom_call_target="tpu_custom_call" | custom-call | flops 20000000000 | bytes 1048576 | tf_op jit(solution)/shard_map/spread_cut/pallas_call | solution.py:141
  66.7 4.2 %all-to-all-start.1 = ((bf16[8,64,256]{2,1,0:T(8,128)(2,1)}), bf16[8,64,256]{2,1,0:T(8,128)(2,1)S(1)}, u32[]{:S(2)}, u32[]{:S(2)}) async-start(bf16[8,64,256]{2,1,0:T(8,128)(2,1)} %bitcast.12), calls=%async_computation.1 | async-start | bytes 524288 | tf_op jit(solution)/shard_map/all_to_all | solution.py:154
  70.8 3.5 %collective-permute-done.2.vd = bf16[128,2048]{1,0:T(8,128)(2,1)} collective-permute-done((bf16[128,2048]{1,0:T(8,128)(2,1)S(1)}, bf16[128,2048]{1,0:T(8,128)(2,1)}, u32[]{:S(2)}, u32[]{:S(2)}) %collective-permute-start.2) | collective-permute-done | bytes 524320 | tf_op jit(solution)/shard_map/ppermute | solution.py:117
  74.3 0.0 copy-done
  74.4 0.0 copy-done.1
  74.4 4.3 %own_factors.1 = (bf16[1024,512]{1,0:T(8,128)(2,1)}, bf16[1024,512]{1,0:T(8,128)(2,1)}, bf16[1024,512]{1,0:T(8,128)(2,1)}, bf16[8,16,256]{2,1,0:T(8,128)(2,1)}) custom-call(s32[9]{0:T(128)S(1)} %stack.35.place, s32[2,8]{1,0:T(2,128)S(1)} %bitcast.18, bf16[3,512,512]{2,1,0:T(8,128)(2,1)S(1)} %copy-done.1, bf16[128,2048]{1,0:T(8,128)(2,1)S(1)} %all_gather.3.ta.tb.tc.td.va, ...), custom_call_target="tpu_custom_call" | custom-call | flops 8000000000 | bytes 8388608 | tf_op jit(solution)/shard_map/own_factors/pallas_call | solution.py:164
  78.6 0.0 all-to-all-done.1.cuts
  78.6 4.2 %tile_cores.1 = f32[8,256,256]{2,1,0:T(8,128)} custom-call(s32[9]{0:T(128)S(1)} %stack.35.place, bf16[3,512,512]{2,1,0:T(8,128)(2,1)S(1)} %copy-done.1, bf16[8,64,256]{2,1,0:T(8,128)(2,1)S(1)} %all-to-all-done.1.cuts, bf16[1024,512]{1,0:T(8,128)(2,1)} %get-tuple-element.13.wt, bf16[1024,512]{1,0:T(8,128)(2,1)} %get-tuple-element.14.lt, ...), custom_call_target="tpu_custom_call" | custom-call | flops 2000000000 | bytes 7340032 | tf_op jit(solution)/shard_map/tile_cores/pallas_call | solution.py:175
Async XLA Ops:
  32.7 32.7 %collective-permute-start.1 = (bf16[128,2048]{1,0:T(8,128)(2,1)S(1)}, bf16[128,2048]{1,0:T(8,128)(2,1)S(1)}, u32[]{:S(2)}, u32[]{:S(2)}) collective-permute-start(bf16[128,2048]{1,0:T(8,128)(2,1)S(1)} %all_gather.3.ta.tb.tc.td.va), channel_id=1, source_target_pairs={{0,16},{1,17},{2,18},{3,19},{4,20},{5,21},{6,22},{7,23},{8,24},{9,... | collective-permute-start | bytes 1572872 | tf_op jit(solution)/shard_map/ppermute | solution.py:117
  35.9 29.5 %collective-permute-start = (bf16[128,2048]{1,0:T(8,128)(2,1)S(1)}, bf16[128,2048]{1,0:T(8,128)(2,1)S(1)}, u32[]{:S(2)}, u32[]{:S(2)}) collective-permute-start(bf16[128,2048]{1,0:T(8,128)(2,1)S(1)} %all_gather.3.ta.tb.tc.td.va), channel_id=1, source_target_pairs={{0,32},{1,33},{2,34},{3,35},{4,36},{5,37},{6,38},{7,39},{8,40},{9,... | collective-permute-start | bytes 1572872 | tf_op jit(solution)/shard_map/ppermute | solution.py:117
  42.5 22.9 %all-to-all-start = ((bf16[32,16,256]{2,1,0:T(8,128)(2,1)}), bf16[32,16,256]{2,1,0:T(8,128)(2,1)S(1)}, u32[]{:S(2)}, u32[]{:S(2)}) async-start(bf16[32,16,256]{2,1,0:T(8,128)(2,1)} %bitcast.11), calls=%async_computation | async-start | bytes 524288 | tf_op jit(solution)/shard_map/all_to_all | solution.py:139
  56.6 17.7 %copy-start = (s32[8,2]{0,1:T(2,128)S(1)}, s32[8,2]{0,1:T(2,128)}, u32[]{:S(2)}) copy-start(s32[8,2]{0,1:T(2,128)} %param.5) | copy-start | bytes 196
  56.6 17.7 %copy-start.1 = (bf16[3,512,512]{2,1,0:T(8,128)(2,1)S(1)}, bf16[3,512,512]{2,1,0:T(8,128)(2,1)}, u32[]{:S(2)}) copy-start(bf16[3,512,512]{2,1,0:T(8,128)(2,1)} %diag.3) | copy-start | bytes 4718596
  56.6 17.7 %collective-permute-start.2 = (bf16[128,2048]{1,0:T(8,128)(2,1)S(1)}, bf16[128,2048]{1,0:T(8,128)(2,1)}, u32[]{:S(2)}, u32[]{:S(2)}) collective-permute-start(bf16[128,2048]{1,0:T(8,128)(2,1)S(1)} %all_gather.3.ta.tb.tc.td.va), channel_id=1, source_target_pairs={{0,48},{1,49},{2,50},{3,51},{4,52},{5,53},{6,54},{7,55},{8,56},{9,... | collective-permute-start | bytes 1572872 | tf_op jit(solution)/shard_map/ppermute | solution.py:117
  66.7 11.9 %all-to-all-start.1 = ((bf16[8,64,256]{2,1,0:T(8,128)(2,1)}), bf16[8,64,256]{2,1,0:T(8,128)(2,1)S(1)}, u32[]{:S(2)}, u32[]{:S(2)}) async-start(bf16[8,64,256]{2,1,0:T(8,128)(2,1)} %bitcast.12), calls=%async_computation.1 | async-start | bytes 524288 | tf_op jit(solution)/shard_map/all_to_all | solution.py:154

commit v7 on v6

--- a/solution.py
+++ b/solution.py
@@ -137,7 +137,7 @@
     )(place, pltpu.with_memory_space_constraint(ranks.T, pltpu.HBM), *[slab] * Y)
     picked = picked.reshape(nrow * Y, rows, wide)
     cut = lax.all_to_all(picked, ("row", "col"), 0, 0, axis_index_groups=across)
-    cut, parts[2], parts[1] = lax.optimization_barrier((cut, parts[2], parts[1]))
+    cut, parts[2] = lax.optimization_barrier((cut, parts[2]))
     sent = pl.pallas_call(
         spread_cut,
         grid_spec=pltpu.PrefetchScalarGridSpec(

time: 83.2 us -> 82.7 us (level)
  starting transfers between devices: 30.6 us -> 28.7 us
  waiting for transfers between devices: 7.65 us -> 8.95 us
    ppermute x3, waiting for transfers between devices: 3.51 us -> 6.74 us  [shards(): lax.ppermute(slab, 'col', [(y * Z + z, (y + d) % Y * Z + z) for y in rang...]
    all_to_all x1, waiting for transfers between devices: 4.14 us -> 2.21 us  [shards(): cut = lax.all_to_all(picked, ('row', 'col'), 0, 0, axis_index_groups=across)]
    ppermute x3, starting transfers between devices: 12.4 us -> 11.4 us  [shards(): lax.ppermute(slab, 'col', [(y * Z + z, (y + d) % Y * Z + z) for y in rang...]
  transfers between devices with their start and end apart: 5 -> 5, of which waited for: 2 -> 3; matrix products, arithmetic and copies ran while one was open for 0% -> 0% of each run, Pallas kernels for 9% -> 9%
where the time goes in v7:
time: 82.7 us; the launch traced here: 82.2 us
  blocking collectives  32.1 us (39%)
  starting transfers between devices  28.7 us (35%)
  Pallas kernels  11.7 us (14%)
  waiting for transfers between devices  8.95 us (11%)
    all_gather x1, blocking collectives, shards(): lax.all_gather(flat, 'col', axis=0, tiled=True, axis_index_groups=along_z)  32.1 us
    all_to_all x1, starting transfers between devices, shards(): cut = lax.all_to_all(picked, ('row', 'col'), 0, 0, axis_index_groups=across)  13.5 us
    ppermute x3, starting transfers between devices, shards(): lax.ppermute(slab, 'col', [(y * Z + z, (y + d) % Y * Z + z) for y in rang...  11.4 us
    ppermute x3, waiting for transfers between devices, shards(): lax.ppermute(slab, 'col', [(y * Z + z, (y + d) % Y * Z + z) for y in rang...  6.74 us
    pallas_call x1, Pallas kernels, shards(): pl.pallas_call(own_factors, grid=(1,), in_specs=[scalars, scalars, matric...  4.26 us
    pallas_call x1, Pallas kernels, shards(): pl.pallas_call(tile_cores, grid=(tiles // some,), in_specs=[scalars, matr...  4.15 us
    all_to_all x1, starting transfers between devices, shards(): cuts = lax.all_to_all(sent.reshape(nrow, Y * rows, wide), 'row', 0, 0)  3.89 us
    all_to_all x1, waiting for transfers between devices, shards(): cut = lax.all_to_all(picked, ('row', 'col'), 0, 0, axis_index_groups=across)  2.21 us
  transfers between devices with their start and end apart: 5, of which 3 were waited for; matrix products, arithmetic and copies ran while one was open for 0% of the time, Pallas kernels for 9%

profile of v7, /device:TPU:1, one launch (start us, length us, event | category | flops | bytes accessed | tf_op | source)
XLA Modules:
  0.0 82.2 jit_solution(6888490820208971571)
XLA Ops:
  0.6 32.1 %all_gather.3.ta.tb.tc.td.va = bf16[128,2048]{1,0:T(8,128)(2,1)S(1)} all-gather(bf16[8,2048]{1,0:T(8,128)(2,1)} %bitcast.19), channel_id=1, replica_groups={{0,1,2,3,4,5,6,7,8,9,10,11,12,13,14,15},{16,17,18,19,20,21,22,23,24,25,..., dimensions={0}, use_global_device_ids=true | all-gather | bytes 557056 | tf_op jit(solution)/shard_map/all_gather | solution.py:115
  32.7 4.8 %collective-permute-start.1 = (bf16[128,2048]{1,0:T(8,128)(2,1)S(1)}, bf16[128,2048]{1,0:T(8,128)(2,1)S(1)}, u32[]{:S(2)}, u32[]{:S(2)}) collective-permute-start(bf16[128,2048]{1,0:T(8,128)(2,1)S(1)} %all_gather.3.ta.tb.tc.td.va), channel_id=1, source_target_pairs={{0,32},{1,33},{2,34},{3,35},{4,36},{5,37},{6,38},{7,39},{8,40},{9,... | collective-permute-start | bytes 1572872 | tf_op jit(solution)/shard_map/ppermute | solution.py:117
  37.6 0.1 stack.35.place
  37.6 2.0 %pick_tiles.1 = bf16[8,4,16,256]{3,2,1,0:T(8,128)(2,1)} custom-call(s32[9]{0:T(128)S(1)} %stack.35.place, s32[2,8]{1,0:T(2,128)} %bitcast.17, bf16[128,2048]{1,0:T(8,128)(2,1)S(1)} %all_gather.3.ta.tb.tc.td.va, bf16[128,2048]{1,0:T(8,128)(2,1)S(1)} %all_gather.3.ta.tb.tc.td.va, bf16[128,2048]{1,0:T(8,128)(2,1)S(1)} %all_gather.3.ta.tb.tc.td.va, ...), custom_call_target="tpu_custom_call" | custom-call | tf_op jit(solution)/shard_map/pick_tiles/pallas_call | solution.py:126
  39.6 13.5 %all-to-all-start = ((bf16[32,16,256]{2,1,0:T(8,128)(2,1)}), bf16[32,16,256]{2,1,0:T(8,128)(2,1)S(1)}, u32[]{:S(2)}, u32[]{:S(2)}) async-start(bf16[32,16,256]{2,1,0:T(8,128)(2,1)} %bitcast.11), calls=%async_computation | async-start | bytes 524288 | tf_op jit(solution)/shard_map/all_to_all | solution.py:139
  53.1 0.0 copy-start
  53.1 0.0 copy-start.1
  53.1 4.6 %collective-permute-start.2 = (bf16[128,2048]{1,0:T(8,128)(2,1)S(1)}, bf16[128,2048]{1,0:T(8,128)(2,1)S(1)}, u32[]{:S(2)}, u32[]{:S(2)}) collective-permute-start(bf16[128,2048]{1,0:T(8,128)(2,1)S(1)} %all_gather.3.ta.tb.tc.td.va), channel_id=1, source_target_pairs={{0,48},{1,49},{2,50},{3,51},{4,52},{5,53},{6,54},{7,55},{8,56},{9,... | collective-permute-start | bytes 1572872 | tf_op jit(solution)/shard_map/ppermute | solution.py:117
  57.8 1.9 %collective-permute-start = (bf16[128,2048]{1,0:T(8,128)(2,1)S(1)}, bf16[128,2048]{1,0:T(8,128)(2,1)}, u32[]{:S(2)}, u32[]{:S(2)}) collective-permute-start(bf16[128,2048]{1,0:T(8,128)(2,1)S(1)} %all_gather.3.ta.tb.tc.td.va), channel_id=1, source_target_pairs={{0,16},{1,17},{2,18},{3,19},{4,20},{5,21},{6,22},{7,23},{8,24},{9,... | collective-permute-start | bytes 1572872 | tf_op jit(solution)/shard_map/ppermute | solution.py:117
  59.7 2.2 %all-to-all-done.cut = bf16[32,16,256]{2,1,0:T(8,128)(2,1)S(1)} async-done(((bf16[32,16,256]{2,1,0:T(8,128)(2,1)}), bf16[32,16,256]{2,1,0:T(8,128)(2,1)S(1)}, u32[]{:S(2)}, u32[]{:S(2)}) %all-to-all-start) | async-done | bytes 262176 | tf_op jit(solution)/shard_map/all_to_all | solution.py:139
  61.9 0.0 collective-permute-done.1.vc
  61.9 1.3 %spread_cut.1 = bf16[8,4,16,256]{3,2,1,0:T(8,128)(2,1)} custom-call(s32[9]{0:T(128)S(1)} %stack.35.place, bf16[32,16,256]{2,1,0:T(8,128)(2,1)S(1)} %all-to-all-done.cut), custom_call_target="tpu_custom_call" | custom-call | flops 20000000000 | bytes 1048576 | tf_op jit(solution)/shard_map/spread_cut/pallas_call | solution.py:141
  63.2 3.9 %all-to-all-start.1 = ((bf16[8,64,256]{2,1,0:T(8,128)(2,1)}), bf16[8,64,256]{2,1,0:T(8,128)(2,1)S(1)}, u32[]{:S(2)}, u32[]{:S(2)}) async-start(bf16[8,64,256]{2,1,0:T(8,128)(2,1)} %bitcast.12), calls=%async_computation.1 | async-start | bytes 524288 | tf_op jit(solution)/shard_map/all_to_all | solution.py:154
  67.1 3.8 %collective-permute-done.2.vd = bf16[128,2048]{1,0:T(8,128)(2,1)S(1)} collective-permute-done((bf16[128,2048]{1,0:T(8,128)(2,1)S(1)}, bf16[128,2048]{1,0:T(8,128)(2,1)S(1)}, u32[]{:S(2)}, u32[]{:S(2)}) %collective-permute-start.2) | collective-permute-done | bytes 524320 | tf_op jit(solution)/shard_map/ppermute | solution.py:117
  70.9 3.0 %collective-permute-done.vb = bf16[128,2048]{1,0:T(8,128)(2,1)} collective-permute-done((bf16[128,2048]{1,0:T(8,128)(2,1)S(1)}, bf16[128,2048]{1,0:T(8,128)(2,1)}, u32[]{:S(2)}, u32[]{:S(2)}) %collective-permute-start) | collective-permute-done | bytes 524320 | tf_op jit(solution)/shard_map/ppermute | solution.py:117
  73.8 0.0 copy-done
  73.8 0.0 copy-done.1
  73.8 4.3 %own_factors.1 = (bf16[1024,512]{1,0:T(8,128)(2,1)}, bf16[1024,512]{1,0:T(8,128)(2,1)}, bf16[1024,512]{1,0:T(8,128)(2,1)}, bf16[8,16,256]{2,1,0:T(8,128)(2,1)}) custom-call(s32[9]{0:T(128)S(1)} %stack.35.place, s32[2,8]{1,0:T(2,128)S(1)} %bitcast.18, bf16[3,512,512]{2,1,0:T(8,128)(2,1)S(1)} %copy-done.1, bf16[128,2048]{1,0:T(8,128)(2,1)S(1)} %all_gather.3.ta.tb.tc.td.va, ...), custom_call_target="tpu_custom_call" | custom-call | flops 8000000000 | bytes 8388608 | tf_op jit(solution)/shard_map/own_factors/pallas_call | solution.py:164
  78.1 0.0 all-to-all-done.1.cuts
  78.1 4.2 %tile_cores.1 = f32[8,256,256]{2,1,0:T(8,128)} custom-call(s32[9]{0:T(128)S(1)} %stack.35.place, bf16[3,512,512]{2,1,0:T(8,128)(2,1)S(1)} %copy-done.1, bf16[8,64,256]{2,1,0:T(8,128)(2,1)S(1)} %all-to-all-done.1.cuts, bf16[1024,512]{1,0:T(8,128)(2,1)} %get-tuple-element.11.wt, bf16[1024,512]{1,0:T(8,128)(2,1)} %get-tuple-element.12.lt, ...), custom_call_target="tpu_custom_call" | custom-call | flops 2000000000 | bytes 7340032 | tf_op jit(solution)/shard_map/tile_cores/pallas_call | solution.py:175
Async XLA Ops:
  32.7 29.2 %collective-permute-start.1 = (bf16[128,2048]{1,0:T(8,128)(2,1)S(1)}, bf16[128,2048]{1,0:T(8,128)(2,1)S(1)}, u32[]{:S(2)}, u32[]{:S(2)}) collective-permute-start(bf16[128,2048]{1,0:T(8,128)(2,1)S(1)} %all_gather.3.ta.tb.tc.td.va), channel_id=1, source_target_pairs={{0,32},{1,33},{2,34},{3,35},{4,36},{5,37},{6,38},{7,39},{8,40},{9,... | collective-permute-start | bytes 1572872 | tf_op jit(solution)/shard_map/ppermute | solution.py:117
  39.6 22.3 %all-to-all-start = ((bf16[32,16,256]{2,1,0:T(8,128)(2,1)}), bf16[32,16,256]{2,1,0:T(8,128)(2,1)S(1)}, u32[]{:S(2)}, u32[]{:S(2)}) async-start(bf16[32,16,256]{2,1,0:T(8,128)(2,1)} %bitcast.11), calls=%async_computation | async-start | bytes 524288 | tf_op jit(solution)/shard_map/all_to_all | solution.py:139
  53.1 20.7 %copy-start = (s32[8,2]{0,1:T(2,128)S(1)}, s32[8,2]{0,1:T(2,128)}, u32[]{:S(2)}) copy-start(s32[8,2]{0,1:T(2,128)} %param.5) | copy-start | bytes 196
  53.1 20.7 %copy-start.1 = (bf16[3,512,512]{2,1,0:T(8,128)(2,1)S(1)}, bf16[3,512,512]{2,1,0:T(8,128)(2,1)}, u32[]{:S(2)}) copy-start(bf16[3,512,512]{2,1,0:T(8,128)(2,1)} %diag.3) | copy-start | bytes 4718596
  53.1 17.7 %collective-permute-start.2 = (bf16[128,2048]{1,0:T(8,128)(2,1)S(1)}, bf16[128,2048]{1,0:T(8,128)(2,1)S(1)}, u32[]{:S(2)}, u32[]{:S(2)}) collective-permute-start(bf16[128,2048]{1,0:T(8,128)(2,1)S(1)} %all_gather.3.ta.tb.tc.td.va), channel_id=1, source_target_pairs={{0,48},{1,49},{2,50},{3,51},{4,52},{5,53},{6,54},{7,55},{8,56},{9,... | collective-permute-start | bytes 1572872 | tf_op jit(solution)/shard_map/ppermute | solution.py:117
  57.8 16.0 %collective-permute-start = (bf16[128,2048]{1,0:T(8,128)(2,1)S(1)}, bf16[128,2048]{1,0:T(8,128)(2,1)}, u32[]{:S(2)}, u32[]{:S(2)}) collective-permute-start(bf16[128,2048]{1,0:T(8,128)(2,1)S(1)} %all_gather.3.ta.tb.tc.td.va), channel_id=1, source_target_pairs={{0,16},{1,17},{2,18},{3,19},{4,20},{5,21},{6,22},{7,23},{8,24},{9,... | collective-permute-start | bytes 1572872 | tf_op jit(solution)/shard_map/ppermute | solution.py:117
  63.2 14.9 %all-to-all-start.1 = ((bf16[8,64,256]{2,1,0:T(8,128)(2,1)}), bf16[8,64,256]{2,1,0:T(8,128)(2,1)S(1)}, u32[]{:S(2)}, u32[]{:S(2)}) async-start(bf16[8,64,256]{2,1,0:T(8,128)(2,1)} %bitcast.12), calls=%async_computation.1 | async-start | bytes 524288 | tf_op jit(solution)/shard_map/all_to_all | solution.py:154
